TPU v7x, 128 devices: a whole 4x4x4 slice. The times are simulated.
128 devices in a mesh: lat: 8 (over y, z_lo), lon: 16 (over z_hi, x, core).
Axes of the slice: x: 4, y: 4, z: 4 (z_hi: 2, z_lo: 2; z = z_hi * 2 + z_lo), core: 2. Of those that a mesh axis runs over, the one named last changes fastest.
Arguments:
- tokens: bfloat16 [64, 768, 512], P('lat', 'lon'), may hold values from -6 to 6
- cotangent: bfloat16 [64, 768, 512], P('lat', 'lon'), may hold values from -6 to 6
- gain_attn: float32 [512], replicated, may hold values from 0.5 to 1.5
- w_qkv: bfloat16 [512, 1536], replicated, may hold values from -3 to 3
- w_proj: bfloat16 [512, 512], replicated, may hold values from -0.25 to 0.25
- rel_table: float32 [8, 225], replicated, may hold values from -4 to 4
- gain_mlp: float32 [512], replicated, may hold values from 0.5 to 1.5
- w_fc1: bfloat16 [512, 2048], replicated, may hold values from -0.25 to 0.25
- w_fc2: bfloat16 [2048, 512], replicated, may hold values from -0.125 to 0.125
Outputs:
- output: bfloat16 [64, 768, 512], P('lat', 'lon')
- grad_tokens: float32 [64, 768, 512], P('lat', 'lon')
- grad_qkv: float32 [512, 1536], P(('lat', 'lon'))
- grad_proj: float32 [512, 512], P(('lat', 'lon'))
- grad_table: float32 [8, 225], replicated
- grad_fc1: float32 [512, 2048], P(('lat', 'lon'))
- grad_fc2: float32 [2048, 512], P(('lat', 'lon'))
- grad_gain_attn: float32 [512], replicated
- grad_gain_mlp: float32 [512], replicated
All inputs are finite; a program needn't handle non-finite values.
Results may differ from a plain program's by a relative error of at most 0.017.
Values may be sent and summed in bfloat16 or wider, within the bound.
A program may use at most 128 MiB of HBM per device.

v0:
```python
import jax
import jax.numpy as jnp
from jax import lax
from jax.experimental import pallas as pl
from jax.experimental.pallas import tpu as pltpu
from jax.sharding import PartitionSpec as P

NORM_EPSILON = 1e-05
D = 512


MESH = pl.DeviceIdType.MESH
F32 = jnp.float32
BF16 = jnp.bfloat16


def place():
    lat = lax.axis_index("lat")
    lon = lax.axis_index("lon")
    return {
        "c": lax.rem(lon, 2),
        "x": lax.rem(lon // 2, 4),
        "y": lat // 2,
        "z": (lon // 8) * 2 + lax.rem(lat, 2),
    }


def moved(at, axis, step):
    size = 2 if axis == "c" else 4
    there = dict(at)
    there[axis] = lax.rem(at[axis] + step, size)
    lat = there["y"] * 2 + lax.rem(there["z"], 2)
    lon = (there["z"] // 2) * 8 + there["x"] * 2 + there["c"]
    return (lat, lon)


class Copies:
    def __init__(self, send_sems, recv_sems):
        self.send_sems, self.recv_sems, self.used = send_sems, recv_sems, 0

    def start(self, src, dst, device):
        copy = pltpu.make_async_remote_copy(
            src_ref=src,
            dst_ref=dst,
            send_sem=self.send_sems.at[self.used],
            recv_sem=self.recv_sems.at[self.used],
            device_id=device,
            device_id_type=MESH,
        )
        self.used += 1
        copy.start()
        return copy


def add_into(target, other, count):
    @pl.loop(0, count)
    def _(i):
        target[i] = (target[i].astype(F32) + other[i].astype(F32)).astype(BF16)


def greet(at, hops, shifts):
    barrier = pltpu.get_barrier_semaphore()
    for step in shifts:
        pl.semaphore_signal(barrier, inc=1, device_id=neighbour(*step), device_id_type=MESH)
    for axis, step in hops:
        pl.semaphore_signal(barrier, inc=1, device_id=moved(at, axis, step), device_id_type=MESH)
    pl.semaphore_wait(barrier, len(hops) + len(shifts))


class Part:
    def __init__(self, at, copies, axes, own, pair, half1, piece1, half2, piece2):
        self.at, self.copies = at, copies
        self.first, self.second = axes
        self.own, self.pair = own, pair
        self.half1, self.piece1, self.half2, self.piece2 = half1, piece1, half2, piece2
        self.rows = own.shape[3]

    def slot(self, step):
        return lax.rem(self.at[self.first] + step, 4)

    def begin(self):
        c = self.at["c"]
        self.pair_copies = {}
        for step in (2, 1, 3, 0):
            j = self.slot(step)
            self.pair_copies[step] = self.copies.start(
                self.own.at[1 - c, j], self.pair.at[j], moved(self.at, "c", 1)
            )

    def pair_sum(self, step):
        self.pair_copies[step].wait()
        j = self.slot(step)
        add_into(self.pair.at[j], self.own.at[self.at["c"], j], 4)

    def first_halves(self):
        self.pair_sum(2)
        j = self.slot(2)
        self.up = self.copies.start(
            self.pair.at[j, 0:2], self.half1.at[0], moved(self.at, self.first, 1)
        )
        self.down = self.copies.start(
            self.pair.at[j, 2:4], self.half1.at[1], moved(self.at, self.first, 3)
        )
        self.pair_sum(1)
        self.pair_sum(3)

    def first_pieces(self):
        self.up.wait()
        add_into(self.pair.at[self.slot(1), 0:2], self.half1.at[0], 2)
        self.up = self.copies.start(
            self.pair.at[self.slot(1)], self.piece1.at[0], moved(self.at, self.first, 1)
        )
        self.down.wait()
        add_into(self.pair.at[self.slot(3), 2:4], self.half1.at[1], 2)
        self.down = self.copies.start(
            self.pair.at[self.slot(3)], self.piece1.at[1], moved(self.at, self.first, 3)
        )
        self.pair_sum(0)

    def second_halves(self):
        self.up.wait()
        self.down.wait()
        mine = self.pair.at[self.slot(0)]

        @pl.loop(0, 4)
        def _(i):
            total = (
                mine[i].astype(F32)
                + self.piece1[0, i].astype(F32)
                + self.piece1[1, i].astype(F32)
            )
            mine[i] = total.astype(BF16)

        k, half = lax.rem(self.at[self.second] + 2, 4), self.rows // 2
        self.up = self.copies.start(
            mine.at[k, 0:half], self.half2.at[0], moved(self.at, self.second, 1)
        )
        self.down = self.copies.start(
            mine.at[k, half : 2 * half], self.half2.at[1], moved(self.at, self.second, 3)
        )

    def second_pieces(self):
        mine, half = self.pair.at[self.slot(0)], self.rows // 2
        k = lax.rem(self.at[self.second] + 1, 4)
        self.up.wait()
        mine[k, 0:half] = (mine[k, 0:half].astype(F32) + self.half2[0].astype(F32)).astype(BF16)
        self.up = self.copies.start(
            mine.at[k], self.piece2.at[0], moved(self.at, self.second, 1)
        )
        k = lax.rem(self.at[self.second] + 3, 4)
        self.down.wait()
        mine[k, half : 2 * half] = (
            mine[k, half : 2 * half].astype(F32) + self.half2[1].astype(F32)
        ).astype(BF16)
        self.down = self.copies.start(
            mine.at[k], self.piece2.at[1], moved(self.at, self.second, 3)
        )

    def finish(self):
        self.up.wait()
        self.down.wait()
        k = self.at[self.second]
        return (
            self.pair[self.slot(0), k].astype(F32)
            + self.piece2[0].astype(F32)
            + self.piece2[1].astype(F32)
        )


def part_scratch(rows, columns=D):
    return [
        pltpu.VMEM((4, 4, rows, columns), BF16),
        pltpu.VMEM((2, 2, rows, columns), BF16),
        pltpu.VMEM((2, 4, rows, columns), BF16),
        pltpu.VMEM((2, rows // 2, columns), BF16),
        pltpu.VMEM((2, rows, columns), BF16),
    ]


def share_all(at, copies, axis, held, slots):
    size = 2 if axis == "c" else 4
    slots[at[axis]] = held[...]
    return [
        copies.start(held, slots.at[at[axis]], moved(at, axis, step)) for step in range(1, size)
    ]


def sum_shared(started, held, slots):
    for copy in started:
        copy.wait()
    total = slots[0]
    for i in range(1, slots.shape[0]):
        total = total + slots[i]
    held[...] = total


def reduce_kernel(
    grad_a, grad_b, small, out_grid, grad_grid,
    qkv_out, proj_out, fc1_out, fc2_out, small_out, output, grad_tokens, *scratch
):
    a_bufs, b_bufs = scratch[0:5], scratch[5:10]
    lines, line_in, held, pair_slots, slots, send_sems, recv_sems = scratch[10:17]
    out_bufs, token_bufs = scratch[17:21], scratch[21:25]
    at = place()
    copies = Copies(send_sems, recv_sems)
    greet(
        at,
        [("c", 1)] + [(axis, step) for axis in ("y", "z", "x") for step in (1, 2, 3)],
        ((1, 0), (0, 1), (1, 1), (-1, 0), (0, -1), (-1, -1)),
    )
    part_a = Part(at, copies, ("y", "z"), grad_a, *a_bufs)
    part_b = Part(at, copies, ("z", "y"), grad_b, *b_bufs)
    held[0] = small[...]
    part_a.begin()
    part_b.begin()
    shared = share_all(at, copies, "c", held.at[0], pair_slots)
    out_rows, out_in, out_edge, out_edge_in = out_bufs
    token_rows, token_in, token_edge, token_edge_in = token_bufs
    back_out = shift_back_start(copies, out_grid, out_rows, out_in, out_edge, out_edge_in)
    back_tokens = shift_back_start(
        copies, grad_grid, token_rows, token_in, token_edge, token_edge_in
    )
    part_a.first_halves()
    part_b.first_halves()
    sum_shared(shared, held.at[1], pair_slots)
    shared = share_all(at, copies, "y", held.at[1], slots.at[0])
    part_a.first_pieces()
    part_b.first_pieces()
    sum_shared(shared, held.at[2], slots.at[0])
    shared = share_all(at, copies, "z", held.at[2], slots.at[1])
    part_a.second_halves()
    part_b.second_halves()
    sum_shared(shared, held.at[3], slots.at[1])
    shared = share_all(at, copies, "x", held.at[3], slots.at[2])
    shift_back_finish(back_out, out_grid, out_in, out_edge_in, output)
    shift_back_finish(back_tokens, grad_grid, token_in, token_edge_in, grad_tokens)
    part_a.second_pieces()
    part_b.second_pieces()
    total_a = part_a.finish()
    total_b = part_b.finish()
    for x in range(4):
        four = slice(4 * x, 4 * x + 4)
        rows = [total_a[64:80][four], total_a[80:96][four], total_b[80:96][four], total_b[64:80][four]]
        rows += [total_b[16 * i : 16 * i + 16][four] for i in range(4)]
        lines[x] = jnp.concatenate(rows + [total_a[16 * x : 16 * x + 16]], axis=0).astype(BF16)
    started = [
        copies.start(
            lines.at[lax.rem(at["x"] + step, 4)], line_in.at[step - 1], moved(at, "x", step)
        )
        for step in (1, 2, 3)
    ]
    total = lines[at["x"]].astype(F32)
    for step in (1, 2, 3):
        started[step - 1].wait()
        total = total + line_in[step - 1].astype(F32)
    for i in range(3):
        qkv_out[:, 512 * i : 512 * i + 512] = total[4 * i : 4 * i + 4]
    proj_out[...] = total[12:16]
    for i in range(4):
        fc1_out[:, 512 * i : 512 * i + 512] = total[16 + 4 * i : 20 + 4 * i]
    fc2_out[...] = total[32:48]
    sum_shared(shared, small_out, slots.at[2])


def reduce_all(grad_a, grad_b, small, out_grid, grad_grid):
    copies = 48
    return pl.pallas_call(
        reduce_kernel,
        out_shape=(
            jax.ShapeDtypeStruct((4, 3 * D), F32),
            jax.ShapeDtypeStruct((4, D), F32),
            jax.ShapeDtypeStruct((4, 4 * D), F32),
            jax.ShapeDtypeStruct((16, D), F32),
            jax.ShapeDtypeStruct((2, 8, D), F32),
            jax.ShapeDtypeStruct((8, 48, D), BF16),
            jax.ShapeDtypeStruct((8, 48, D), F32),
        ),
        in_specs=[pl.BlockSpec(memory_space=pltpu.VMEM)] * 5,
        out_specs=[pl.BlockSpec(memory_space=pltpu.VMEM)] * 7,
        scratch_shapes=part_scratch(96)
        + part_scratch(96)
        + [
            pltpu.VMEM((4, 48, D), BF16),
            pltpu.VMEM((3, 48, D), BF16),
            pltpu.VMEM((4, 2, 8, D), F32),
            pltpu.VMEM((2, 2, 8, D), F32),
            pltpu.VMEM((3, 4, 2, 8, D), F32),
            pltpu.SemaphoreType.DMA((copies,)),
            pltpu.SemaphoreType.DMA((copies,)),
        ]
        + ([pltpu.VMEM((4, 48, D), BF16)] + SHIFT_SCRATCH) * 2,
        compiler_params=pltpu.CompilerParams(
            collective_id=0, has_side_effects=True, vmem_limit_bytes=56 * 2**20
        ),
        name="reduce_grads",
    )(grad_a, grad_b, small, out_grid, grad_grid)


def neighbour(step_lat, step_lon):
    return (
        lax.rem(lax.axis_index("lat") + step_lat + 8, 8),
        lax.rem(lax.axis_index("lon") + step_lon + 16, 16),
    )


def greet_shift():
    barrier = pltpu.get_barrier_semaphore()
    steps = ((1, 0), (0, 1), (1, 1), (-1, 0), (0, -1), (-1, -1))
    for step in steps:
        pl.semaphore_signal(barrier, inc=1, device_id=neighbour(*step), device_id_type=MESH)
    pl.semaphore_wait(barrier, len(steps))


def shift_in_start(copies, source, rows_in, edge, edge_in):
    started = [copies.start(source.at[4:8], rows_in, neighbour(1, 0))]
    for half in range(2):
        ends = [source[4 * half + r, 32:48].astype(F32)[12:16] for r in range(4)]
        edge[half] = jnp.concatenate(ends, axis=0).astype(BF16)
    started.append(copies.start(edge.at[0], edge_in.at[0], neighbour(0, 1)))
    started.append(copies.start(edge.at[1], edge_in.at[1], neighbour(1, 1)))
    return started


def shift_in_finish(started, source, rows_in, edge_in, grid):
    for copy in started:
        copy.wait()
    for row in range(8):
        held = (rows_in[row] if row < 4 else source[row - 4]).astype(F32)
        turned = pltpu.roll(held, 4, 0)
        ends = edge_in[1 if row < 4 else 0].astype(F32)[4 * (row % 4) : 4 * (row % 4) + 4]
        grid[row] = jnp.concatenate(
            [jnp.concatenate([ends, turned[4:8]], axis=0), turned[8:48]], axis=0
        )


def shift_back_start(copies, grid, rows_out, rows_in, edge, edge_in):
    for row in range(4):
        rows_out[row] = pltpu.roll(grid[row], 44, 0).astype(BF16)
    started = [copies.start(rows_out, rows_in, neighbour(-1, 0))]
    for half in range(2):
        firsts = [grid[4 * half + r, 0:8][0:4] for r in range(4)]
        edge[half] = jnp.concatenate(firsts, axis=0).astype(BF16)
    started.append(copies.start(edge.at[1], edge_in.at[1], neighbour(0, -1)))
    started.append(copies.start(edge.at[0], edge_in.at[0], neighbour(-1, -1)))
    return started


def shift_back_finish(started, grid, rows_in, edge_in, result):
    for copy in started:
        copy.wait()
    for row in range(8):
        if row < 4:
            turned = pltpu.roll(grid[row + 4], 44, 0)
        else:
            turned = rows_in[row - 4].astype(F32)
        ends = edge_in[1 if row < 4 else 0].astype(F32)[4 * (row % 4) : 4 * (row % 4) + 4]
        whole = jnp.concatenate(
            [turned[0:40], jnp.concatenate([turned[40:44], ends], axis=0)], axis=0
        )
        result[row] = whole.astype(result.dtype)


SHIFT_SCRATCH = [
    pltpu.VMEM((4, 48, D), BF16),
    pltpu.VMEM((2, 16, D), BF16),
    pltpu.VMEM((2, 16, D), BF16),
]


def shift_kernel(tokens, cotangent, x_grid, c_grid, *scratch):
    copies = Copies(*scratch[6:])
    greet_shift()
    started = []
    for source, bufs in ((tokens, scratch[0:3]), (cotangent, scratch[3:6])):
        started.append(shift_in_start(copies, source, *bufs))
    for source, bufs, grid, copied in (
        (tokens, scratch[0:3], x_grid, started[0]),
        (cotangent, scratch[3:6], c_grid, started[1]),
    ):
        shift_in_finish(copied, source, bufs[0], bufs[2], grid)


def shift_in(tokens, cotangent):
    vmem = pl.BlockSpec(memory_space=pltpu.VMEM)
    return pl.pallas_call(
        shift_kernel,
        out_shape=(jax.ShapeDtypeStruct((8, 48, D), F32),) * 2,
        in_specs=[vmem] * 2,
        out_specs=[vmem] * 2,
        scratch_shapes=SHIFT_SCRATCH * 2
        + [pltpu.SemaphoreType.DMA((6,)), pltpu.SemaphoreType.DMA((6,))],
        compiler_params=pltpu.CompilerParams(
            collective_id=1, has_side_effects=True, vmem_limit_bytes=56 * 2**20
        ),
        name="shift_in",
    )(tokens, cotangent)


TOKENS = 384
WINDOWS = 6
PAIRS = 4
TILE = 16


def mm(a, b):
    return lax.dot_general(a, b, (((1,), (0,)), ((), ())), preferred_element_type=F32)


def mm_nt(a, b):
    return lax.dot_general(a, b, (((1,), (1,)), ((), ())), preferred_element_type=F32)


def mm_tn(a, b):
    return lax.dot_general(a, b, (((0,), (0,)), ((), ())), preferred_element_type=F32)


def split_low(value):
    high = value.astype(BF16)
    return high, (value - high.astype(F32)).astype(BF16)


def iota(shape, dim):
    return lax.broadcasted_iota(jnp.int32, shape, dim)


def tiles(body):
    @pl.loop(0, TOKENS // TILE)
    def _(i):
        body(i, pl.ds(pl.multiple_of(i * TILE, TILE), TILE))


def grid_tile(grid, i):
    window, row = i // 4, lax.rem(i, 4) * 2
    columns = pl.ds(pl.multiple_of(window * 8, 8), 8)
    return jnp.concatenate([grid[row, columns], grid[row + 1, columns]], axis=0)


def store_grid_tile(grid, i, tile):
    window, row = i // 4, lax.rem(i, 4) * 2
    columns = pl.ds(pl.multiple_of(window * 8, 8), 8)
    grid[row, columns] = tile[0:8]
    grid[row + 1, columns] = tile[8:16]


def normalise(vectors):
    centred = vectors - jnp.mean(vectors, axis=-1, keepdims=True)
    factor = lax.rsqrt(jnp.mean(centred * centred, axis=-1, keepdims=True) + NORM_EPSILON)
    return centred * factor, factor


def normalise_back(grad_out, normal, factor, gain):
    grad_hat = grad_out * gain
    inner = (
        grad_hat
        - jnp.mean(grad_hat, axis=-1, keepdims=True)
        - normal * jnp.mean(grad_hat * normal, axis=-1, keepdims=True)
    )
    return factor * inner


def line_order(first_z):
    place_of = iota((1, D), 1)
    core, first, second = place_of >> 8, (place_of >> 6) & 3, (place_of >> 4) & 3
    x, r = (place_of >> 2) & 3, place_of & 3
    y, z = (second, first) if first_z else (first, second)
    feature = (y << 7) | ((z & 1) << 6) | ((z >> 1) << 5) | (x << 3) | (core << 2) | r
    return jnp.where(iota((D, D), 0) == feature, 1.0, 0.0).astype(BF16)


def pair_offsets():
    row, column = iota((256, 128), 0), iota((256, 128), 1)
    target = ((column >> 6) << 7) + 15 * ((column >> 3) & 7) + (column & 7)
    return jnp.where(row == target, 1.0, 0.0).astype(BF16)


def store_wide(halves, i, rows):
    halves[0, 8 * i : 8 * i + 8] = rows[:, 0:128]
    halves[1, 8 * i : 8 * i + 8] = rows[:, 128:256]


def load_strided(halves, first):
    return jnp.concatenate([halves[k, pl.ds(first, 8, stride=8), :] for k in range(2)], axis=1)


def expand_bias(rel, table, shifted, bias, masked):
    table[...] = jnp.zeros_like(table)
    table[:, 0:225] = rel[...]
    whole = table[...]
    for b in range(8):
        store_wide(shifted, b, pltpu.roll(whole, (256 - (7 - b)) % 256, 1))
    spread = pair_offsets()
    key, query = iota((64, 128), 0), iota((64, 128), 1) & 63
    apart = jnp.where((key >> 5) == (query >> 5), 0.0, -1e30)
    apart = jnp.where(masked, apart, 0.0)
    for p in range(PAIRS):
        heads = []
        for h in (2 * p, 2 * p + 1):
            rows = load_strided(shifted, h)
            turned = [pltpu.roll(rows, 256 - (105 - 15 * a), 1)[:, 0:128] for a in range(8)]
            heads.append(jnp.concatenate(turned, axis=0))
        high, low = split_low(jnp.concatenate(heads, axis=1))
        bias[p] = mm(high, spread) + mm(low, spread) + apart


def collect_table(grad_bias, collected, total):
    spread = pair_offsets()
    for p in range(PAIRS):
        high, low = split_low(grad_bias[p])
        both = mm_nt(high, spread) + mm_nt(low, spread)
        for k in range(2):
            one = both[:, 128 * k : 128 * k + 128]
            one = jnp.concatenate([one, jnp.zeros_like(one)], axis=1)
            rows = one[56:64]
            for a in range(7):
                rows = rows + pltpu.roll(one[8 * a : 8 * a + 8], 105 - 15 * a, 1)
            h = 2 * p + k
            store_wide(collected, h, rows)
    table = load_strided(collected, 7)
    for b in range(7):
        table = table + pltpu.roll(load_strided(collected, b), 7 - b, 1)
    total[...] = table


def both_heads(pair):
    left = iota(pair.shape, 1) < 64
    zero = jnp.zeros_like(pair)
    return jnp.concatenate([jnp.where(left, pair, zero), jnp.where(left, zero, pair)], axis=0)


def own_heads(crossed):
    return jnp.where(iota((64, 128), 1) < 64, crossed[0:64], crossed[64:128])


def window_rows(w):
    return pl.ds(pl.multiple_of(w * 64, 64), 64)


def attend(w, qkv, bias, probs, attended):
    rows = window_rows(w)
    for p in range(PAIRS):
        query = qkv[rows, 128 * p : 128 * p + 128]
        keys = qkv[rows, D + 128 * p : D + 128 * p + 128]
        values = qkv[rows, 2 * D + 128 * p : 2 * D + 128 * p + 128]
        scores = mm_nt(keys, both_heads(query)) + bias[p]
        powers = jnp.exp(scores - jnp.max(scores, axis=0, keepdims=True))
        each = powers / jnp.sum(powers, axis=0, keepdims=True)
        probs[w, p] = each
        crossed = mm_tn(each.astype(BF16), values)
        attended[rows, 128 * p : 128 * p + 128] = own_heads(crossed).astype(BF16)


def attend_back(w, qkv, probs, grad_attended, grad_bias, grad_rows):
    rows = window_rows(w)
    for p in range(PAIRS):
        query = both_heads(qkv[rows, 128 * p : 128 * p + 128])
        keys = qkv[rows, D + 128 * p : D + 128 * p + 128]
        values = qkv[rows, 2 * D + 128 * p : 2 * D + 128 * p + 128]
        grads = both_heads(grad_attended[rows, 128 * p : 128 * p + 128])
        each = probs[w, p]
        grad_probs = mm_nt(values, grads)
        grad_scores = each * (grad_probs - jnp.sum(each * grad_probs, axis=0, keepdims=True))
        grad_bias[p] += grad_scores
        low = grad_scores.astype(BF16)
        grad_query = own_heads(mm_tn(low, keys)) * 0.125
        grad_rows[rows, 128 * p : 128 * p + 128] = grad_query.astype(BF16)
        grad_rows[rows, D + 128 * p : D + 128 * p + 128] = mm(low, query).astype(BF16)
        grad_rows[rows, 2 * D + 128 * p : 2 * D + 128 * p + 128] = mm(
            each.astype(BF16), grads
        ).astype(BF16)


GELU_SCALE = 0.7978845608028654
GELU_CUBE = 0.044715


def gelu_both(hidden):
    square = hidden * hidden
    swing = jnp.tanh(GELU_SCALE * hidden * (1.0 + GELU_CUBE * square))
    half = 0.5 + 0.5 * swing
    slope = half + (0.5 * GELU_SCALE) * hidden * (1.0 - swing * swing) * (
        1.0 + 3.0 * GELU_CUBE * square
    )
    return hidden * half, slope


def eight(tile):
    return tile[0:8] + tile[8:16]


COMPUTE_SCRATCH = [
    ("hat1", (TOKENS, D), F32),
    ("factor1", (TOKENS, 128), F32),
    ("norm1", (TOKENS, D), BF16),
    ("qkv", (TOKENS, 3 * D), BF16),
    ("attended", (TOKENS, D), BF16),
    ("resid", (TOKENS, D), F32),
    ("hat2", (TOKENS, D), F32),
    ("factor2", (TOKENS, 128), F32),
    ("norm2", (TOKENS, D), BF16),
    ("norm2_z", (TOKENS, D), BF16),
    ("cot", (TOKENS, D), BF16),
    ("hidden", (TOKENS, D), F32),
    ("grad_active", (TOKENS, D), F32),
    ("active", (TOKENS, D), BF16),
    ("grad_hidden", (TOKENS, D), BF16),
    ("mlp_out", (TOKENS, D), F32),
    ("grad_norm", (TOKENS, D), F32),
    ("grad_resid", (TOKENS, D), F32),
    ("grad_resid_low", (TOKENS, D), BF16),
    ("grad_attended", (TOKENS, D), BF16),
    ("grad_rows", (TOKENS, 3 * D), BF16),
    ("probs", (WINDOWS, PAIRS, 64, 128), F32),
    ("bias", (PAIRS, 64, 128), F32),
    ("grad_bias", (PAIRS, 64, 128), F32),
    ("table", (8, 256), F32),
    ("shifted", (2, 64, 128), F32),
    ("gain_sums", (2, 8, D), F32),
]


class Block:
    def __init__(self, refs):
        for (name, _, _), ref in zip(COMPUTE_SCRATCH, refs):
            setattr(self, name, ref)


def attention_forward(s, x_grid, gain_attn, w_qkv, rel, masked):
    expand_bias(rel, s.table, s.shifted, s.bias, masked)

    def first_norm(i, rows):
        normal, factor = normalise(grid_tile(x_grid, i))
        s.hat1[rows] = normal
        s.factor1[rows] = jnp.broadcast_to(factor, (TILE, 128))
        s.norm1[rows] = (normal * gain_attn[...]).astype(BF16)

    tiles(first_norm)
    for i in range(3):
        columns = slice(D * i, D * i + D)
        part = mm(s.norm1[...], w_qkv[:, columns])
        s.qkv[:, columns] = (part * 0.125 if i == 0 else part).astype(BF16)

    @pl.loop(0, WINDOWS)
    def _(w):
        attend(w, s.qkv, s.bias, s.probs, s.attended)


def mlp(s, x_grid, c_grid, w_proj, gain_mlp, w_fc1, w_fc2, out_grid, grad_a, grad_b, each=None):
    s.resid[...] = mm(s.attended[...], w_proj[...])

    def second_norm(i, rows):
        resid = s.resid[rows] + grid_tile(x_grid, i)
        normal, factor = normalise(resid)
        s.resid[rows] = resid
        s.hat2[rows] = normal
        s.factor2[rows] = jnp.broadcast_to(factor, (TILE, 128))
        s.norm2[rows] = (normal * gain_mlp[...]).astype(BF16)
        s.cot[rows] = grid_tile(c_grid, i).astype(BF16)

    tiles(second_norm)
    s.norm2_z[...] = mm(s.norm2[...], line_order(True)).astype(BF16)
    s.mlp_out[...] = jnp.zeros_like(s.mlp_out)
    s.grad_norm[...] = jnp.zeros_like(s.grad_norm)

    @pl.loop(0, 4)
    def _(j):
        columns = pl.ds(pl.multiple_of(j * D, D), D)
        s.hidden[...] = mm(s.norm2[...], w_fc1[:, columns])
        s.grad_active[...] = mm_nt(s.cot[...], w_fc2[columns])

        def bend(_, rows):
            active, slope = gelu_both(s.hidden[rows])
            s.active[rows] = active.astype(BF16)
            s.grad_hidden[rows] = (slope * s.grad_active[rows]).astype(BF16)

        tiles(bend)
        s.mlp_out[...] += mm(s.active[...], w_fc2[columns])
        s.grad_norm[...] += mm_nt(s.grad_hidden[...], w_fc1[:, columns])
        grad_fc1 = mm_tn(s.norm2_z[...], s.grad_hidden[...]).astype(BF16)
        grad_b[:, :, :, pl.ds(pl.multiple_of(j * 16, 16), 16), :] = grad_fc1.reshape(2, 4, 4, 16, D)
        grad_fc2 = mm_tn(s.active[...], s.cot[...]).astype(BF16).reshape(2, 2, 4, 2, 16, D)
        for low in range(2):
            for high in range(2):
                for x in range(4):
                    for c in range(2):
                        grad_a[c, j, 2 * high + low, 16 * x : 16 * x + 16, :] = grad_fc2[
                            low, high, x, c
                        ]

    s.gain_sums[...] = jnp.zeros_like(s.gain_sums)

    def second_back(i, rows):
        grad, normal = s.grad_norm[rows], s.hat2[rows]
        s.gain_sums[1] += eight(grad * normal)
        grad_resid = s.cot[rows].astype(F32) + normalise_back(
            grad, normal, s.factor2[rows][:, 0:1], gain_mlp[...]
        )
        s.grad_resid[rows] = grad_resid
        s.grad_resid_low[rows] = grad_resid.astype(BF16)
        store_grid_tile(out_grid, i, s.resid[rows] + s.mlp_out[rows])

    tiles(second_back)


def attention_backward(s, gain_attn, w_qkv, w_proj, grad_grid, grad_a, grad_b, small):
    by_z = line_order(True)
    s.norm2_z[...] = mm(s.attended[...], by_z).astype(BF16)
    grad_proj = mm_tn(s.norm2_z[...], s.grad_resid_low[...]).astype(BF16)
    grad_b[:, :, :, 64:80, :] = grad_proj.reshape(2, 4, 4, 16, D)
    s.grad_attended[...] = mm_nt(s.grad_resid_low[...], w_proj[...]).astype(BF16)
    s.grad_bias[...] = jnp.zeros_like(s.grad_bias)

    @pl.loop(0, WINDOWS)
    def _(w):
        attend_back(w, s.qkv, s.probs, s.grad_attended, s.grad_bias, s.grad_rows)

    s.norm2_z[...] = mm(s.norm1[...], by_z).astype(BF16)
    grad_values = mm_tn(s.norm2_z[...], s.grad_rows[:, 2 * D : 3 * D]).astype(BF16)
    grad_b[:, :, :, 80:96, :] = grad_values.reshape(2, 4, 4, 16, D)
    s.norm2_z[...] = mm(s.norm1[...], line_order(False)).astype(BF16)
    for i in range(2):
        grad = mm_tn(s.norm2_z[...], s.grad_rows[:, D * i : D * i + D]).astype(BF16)
        grad_a[:, :, :, 64 + 16 * i : 80 + 16 * i, :] = grad.reshape(2, 4, 4, 16, D)
    s.grad_norm[...] = mm_nt(s.grad_rows[...], w_qkv[...])

    def first_back(i, rows):
        grad, normal = s.grad_norm[rows], s.hat1[rows]
        s.gain_sums[0] += eight(grad * normal)
        store_grid_tile(
            grad_grid,
            i,
            s.grad_resid[rows]
            + normalise_back(grad, normal, s.factor1[rows][:, 0:1], gain_attn[...]),
        )

    tiles(first_back)
    collect_table(s.grad_bias, s.shifted, s.table)
    small[...] = jnp.zeros_like(small)
    small[0, 0:1] = jnp.sum(s.gain_sums[0], axis=0, keepdims=True)
    small[0, 1:2] = jnp.sum(s.gain_sums[1], axis=0, keepdims=True)
    small[1, :, 0:256] = s.table[...]


def compute_kernel(
    x_grid, c_grid, gain_attn, w_qkv, w_proj, rel, gain_mlp, w_fc1, w_fc2,
    out_grid, grad_grid, grad_a, grad_b, small, *scratch
):
    s = Block(scratch)
    attention_forward(s, x_grid, gain_attn, w_qkv, rel, lax.axis_index("lat") == 0)
    mlp(s, x_grid, c_grid, w_proj, gain_mlp, w_fc1, w_fc2, out_grid, grad_a, grad_b)
    attention_backward(s, gain_attn, w_qkv, w_proj, grad_grid, grad_a, grad_b, small)


def compute(x_grid, c_grid, gain_attn, w_qkv, w_proj, rel, gain_mlp, w_fc1, w_fc2):
    vmem = pl.BlockSpec(memory_space=pltpu.VMEM)
    return pl.pallas_call(
        compute_kernel,
        out_shape=(
            jax.ShapeDtypeStruct((8, 48, D), F32),
            jax.ShapeDtypeStruct((8, 48, D), F32),
            jax.ShapeDtypeStruct((2, 4, 4, 96, D), BF16),
            jax.ShapeDtypeStruct((2, 4, 4, 96, D), BF16),
            jax.ShapeDtypeStruct((2, 8, D), F32),
        ),
        in_specs=[vmem] * 9,
        out_specs=[vmem] * 5,
        scratch_shapes=[pltpu.VMEM(shape, kind) for _, shape, kind in COMPUTE_SCRATCH],
        compiler_params=pltpu.CompilerParams(vmem_limit_bytes=56 * 2**20),
        name="block",
    )(x_grid, c_grid, gain_attn.reshape(1, D), w_qkv, w_proj, rel, gain_mlp.reshape(1, D), w_fc1, w_fc2)


def shards(tokens, cotangent, gain_attn, w_qkv, w_proj, rel_table, gain_mlp, w_fc1, w_fc2):
    x_grid, c_grid = shift_in(tokens, cotangent)
    out_grid, grad_grid, grad_a, grad_b, small = compute(
        x_grid, c_grid, gain_attn, w_qkv, w_proj, rel_table, gain_mlp, w_fc1, w_fc2
    )
    grad_qkv, grad_proj, grad_fc1, grad_fc2, small, output, grad_tokens = reduce_all(
        grad_a, grad_b, small, out_grid, grad_grid
    )
    return (
        output,
        grad_tokens,
        grad_qkv,
        grad_proj,
        small[1, :, :225],
        grad_fc1,
        grad_fc2,
        small[0, 0],
        small[0, 1],
    )


def solution(mesh):
    placed = (P("lat", "lon", None), P("lat", "lon", None), P(), P(), P(), P(), P(), P(), P())
    return jax.shard_map(
        shards,
        mesh=mesh,
        in_specs=placed,
        out_specs=(
            P("lat", "lon", None),
            P("lat", "lon", None),
            P(("lat", "lon"), None),
            P(("lat", "lon"), None),
            P(),
            P(("lat", "lon"), None),
            P(("lat", "lon"), None),
            P(),
            P(),
        ),
        check_vma=False,
    )
```

profile of v0, /device:TPU:0, one launch (start us, length us, event | category | flops | bytes accessed | tf_op | source)
XLA Modules:
  0.0 123.3 jit_solution(6165763888291619522)
XLA Ops:
  0.6 18.5 %shift_in.1 = (f32[8,48,512]{2,1,0:T(8,128)}, f32[8,48,512]{2,1,0:T(8,128)}) custom-call(bf16[8,48,512]{2,1,0:T(8,128)(2,1)} %tokens.1, bf16[8,48,512]{2,1,0:T(8,128)(2,1)} %cotangent.1), custom_call_target="tpu_custom_call" | custom-call | tf_op jit(solution)/shard_map/shift_in/pallas_call | solution.py:385
  19.1 46.4 %block.1 = (f32[8,48,512]{2,1,0:T(8,128)}, f32[8,48,512]{2,1,0:T(8,128)}, bf16[2,4,4,96,512]{4,3,2,1,0:T(8,128)(2,1)}, bf16[2,4,4,96,512]{4,3,2,1,0:T(8,128)(2,1)}, f32[2,8,512]{2,1,0:T(8,128)}) custom-call(f32[8,48,512]{2,1,0:T(8,128)} %get-tuple-element.23.x_grid, f32[8,48,512]{2,1,0:T(8,128)} %get-tuple-element.24.c_grid, f32[1,512]{1,0:T(1,128)} %bitcast.8, ...), custom_call_target="tpu_custom_call" | custom-call | tf_op jit(solution)/shard_map/block/pallas_call | solution.py:755
  65.5 48.8 %reduce_grads.1 = (f32[4,1536]{1,0:T(4,128)}, f32[4,512]{1,0:T(4,128)}, f32[4,2048]{1,0:T(4,128)}, f32[16,512]{1,0:T(8,128)}, f32[2,8,512]{2,1,0:T(8,128)}, /*in...) custom-call(bf16[2,4,4,96,512]{4,3,2,1,0:T(8,128)(2,1)} %get-tuple-element.25.grad_a, ...), custom_call_target="tpu_custom_call" | custom-call | tf_op jit(solution)/shard_map/reduce_grads/pallas_call | solution.py:267
  114.3 0.0 copy-start.2
  114.3 0.0 copy-start.3
  114.3 0.0 copy-start.1
  114.3 0.0 copy-start
  114.3 1.4 %fusion = (f32[1,1,512]{2,1,0:T(1,128)}, f32[1,1,512]{2,1,0:T(1,128)}) fusion(f32[2,8,512]{2,1,0:T(8,128)} %get-tuple-element.34), kind=kLoop, calls=%fused_computation.1 | loop fusion | bytes 8192 | tf_op jit(solution)/shard_map/slice | solution.py:789
  115.7 1.3 %slice_bitcast_fusion = f32[8,225]{1,0:T(8,128)} fusion(f32[2,8,512]{2,1,0:T(8,128)} %get-tuple-element.34), kind=kLoop, calls=%fused_computation | loop fusion | bytes 14400 | tf_op jit(solution)/shard_map/squeeze | solution.py:785
  117.0 1.8 %copy.24 = bf16[8,48,512]{2,1,0:T(8,128)(2,1)} copy(bf16[8,48,512]{2,1,0:T(8,128)(2,1)} %get-tuple-element.48) | data formatting | bytes 786432
  118.8 2.1 %copy.25 = f32[8,48,512]{2,1,0:T(8,128)} copy(f32[8,48,512]{2,1,0:T(8,128)} %get-tuple-element.49) | data formatting | bytes 1572864
  120.8 0.0 copy-done.2
  120.8 0.6 copy.26
  121.4 0.0 copy-done.3
  121.4 0.6 copy.27
  122.0 0.0 copy-done.1
  122.0 0.6 copy.28
  122.7 0.0 copy-done
  122.7 0.6 copy.29
Async XLA Ops:
  114.3 6.5 %copy-start.2 = (f32[4,1536]{1,0:T(4,128)S(1)}, f32[4,1536]{1,0:T(4,128)}, u32[]{:S(2)}) copy-start(f32[4,1536]{1,0:T(4,128)} %get-tuple-element.50) | copy-start | bytes 73732
  114.3 7.1 %copy-start.3 = (f32[4,512]{1,0:T(4,128)S(1)}, f32[4,512]{1,0:T(4,128)}, u32[]{:S(2)}) copy-start(f32[4,512]{1,0:T(4,128)} %get-tuple-element.51) | copy-start | bytes 24580
  114.3 7.7 %copy-start.1 = (f32[4,2048]{1,0:T(4,128)S(1)}, f32[4,2048]{1,0:T(4,128)}, u32[]{:S(2)}) copy-start(f32[4,2048]{1,0:T(4,128)} %get-tuple-element.53) | copy-start | bytes 98308
  114.3 8.3 %copy-start = (f32[16,512]{1,0:T(8,128)S(1)}, f32[16,512]{1,0:T(8,128)}, u32[]{:S(2)}) copy-start(f32[16,512]{1,0:T(8,128)} %get-tuple-element.54) | copy-start | bytes 98308
where the time goes:
time: 124 us; the launch traced here: 123 us
  Pallas kernels  114 us (92%)
  local copies, waits for them, and re-layouts  8.96 us (7%)
    pallas_call x1, Pallas kernels, reduce_all(): pl.pallas_call(reduce_kernel, out_shape=(jax.ShapeDtypeStruct((4, 3 * D),...  48.8 us
    pallas_call x1, Pallas kernels, compute(): pl.pallas_call(compute_kernel, out_shape=(jax.ShapeDtypeStruct((8, 48, D)...  46.4 us
    pallas_call x1, Pallas kernels, shift_in(): pl.pallas_call(shift_kernel, out_shape=(jax.ShapeDtypeStruct((8, 48, D),...  18.5 us
    unnamed x14, local copies, waits for them, and re-layouts  6.28 us

commit v1 on v0

v1 whole, which is shorter than its diff:
```python
import jax
import jax.numpy as jnp
from jax import lax
from jax.experimental import pallas as pl
from jax.experimental.pallas import tpu as pltpu
from jax.sharding import PartitionSpec as P

NORM_EPSILON = 1e-05
D = 512


MESH = pl.DeviceIdType.MESH
F32 = jnp.float32
BF16 = jnp.bfloat16


def place():
    lat = lax.axis_index("lat")
    lon = lax.axis_index("lon")
    return {
        "c": lax.rem(lon, 2),
        "x": lax.rem(lon // 2, 4),
        "y": lat // 2,
        "z": (lon // 8) * 2 + lax.rem(lat, 2),
    }


def moved(at, axis, step):
    size = 2 if axis == "c" else 4
    there = dict(at)
    there[axis] = lax.rem(at[axis] + step, size)
    lat = there["y"] * 2 + lax.rem(there["z"], 2)
    lon = (there["z"] // 2) * 8 + there["x"] * 2 + there["c"]
    return (lat, lon)


def neighbour(step_lat, step_lon):
    return (
        lax.rem(lax.axis_index("lat") + step_lat + 8, 8),
        lax.rem(lax.axis_index("lon") + step_lon + 16, 16),
    )


def greet(at):
    barrier = pltpu.get_barrier_semaphore()
    others = [moved(at, "c", 1)]
    others += [moved(at, axis, step) for axis in ("y", "z", "x") for step in (1, 2, 3)]
    steps = ((1, 0), (0, 1), (1, 1), (-1, 0), (0, -1), (-1, -1))
    others += [neighbour(*step) for step in steps]
    for other in others:
        pl.semaphore_signal(barrier, inc=1, device_id=other, device_id_type=MESH)
    pl.semaphore_wait(barrier, len(others))


class Copies:
    def __init__(self, send_sems, recv_sems):
        self.send_sems, self.recv_sems, self.used = send_sems, recv_sems, 0

    def reserve(self, count):
        self.used += count
        return self.used - count

    def make(self, index, src, dst, device):
        return pltpu.make_async_remote_copy(
            src_ref=src,
            dst_ref=dst,
            send_sem=self.send_sems.at[index],
            recv_sem=self.recv_sems.at[index],
            device_id=device,
            device_id_type=MESH,
        )

    def start(self, src, dst, device):
        copy = self.make(self.reserve(1), src, dst, device)
        copy.start()
        return copy


def add_into(target, other, count):
    @pl.loop(0, count)
    def _(i):
        target[i] = (target[i].astype(F32) + other[i].astype(F32)).astype(BF16)


class Part:
    def __init__(self, at, copies, axes, own, pair, half1, piece1, piece2):
        self.at, self.copies = at, copies
        self.first, self.second = axes
        self.own, self.pair = own, pair
        self.half1, self.piece1, self.piece2 = half1, piece1, piece2
        self.base = copies.reserve(4)

    def slot(self, step):
        return lax.rem(self.at[self.first] + step, 4)

    def pair_copy(self, i):
        j = self.slot(6 - i)
        return self.copies.make(
            self.base + i, self.own.at[1 - self.at["c"], j], self.pair.at[j], moved(self.at, "c", 1)
        )

    def begin(self):
        for i in range(4):
            self.pair_copy(i).start()

    def pair_sum(self, i):
        self.pair_copy(i).wait()
        j = self.slot(6 - i)
        add_into(self.pair.at[j], self.own.at[self.at["c"], j], 4)

    def first_halves(self):
        self.pair_sum(0)
        j = self.slot(2)
        self.up = self.copies.start(
            self.pair.at[j, 0:2], self.half1.at[0], moved(self.at, self.first, 1)
        )
        self.down = self.copies.start(
            self.pair.at[j, 2:4], self.half1.at[1], moved(self.at, self.first, 3)
        )
        self.pair_sum(1)
        self.pair_sum(3)

    def first_pieces(self):
        self.up.wait()
        add_into(self.pair.at[self.slot(1), 0:2], self.half1.at[0], 2)
        self.up = self.copies.start(
            self.pair.at[self.slot(1)], self.piece1.at[0], moved(self.at, self.first, 1)
        )
        self.down.wait()
        add_into(self.pair.at[self.slot(3), 2:4], self.half1.at[1], 2)
        self.down = self.copies.start(
            self.pair.at[self.slot(3)], self.piece1.at[1], moved(self.at, self.first, 3)
        )
        self.pair_sum(2)

    def second_send(self):
        self.up.wait()
        self.down.wait()
        mine = self.pair.at[self.slot(0)]

        @pl.loop(0, 4)
        def _(i):
            total = (
                mine[i].astype(F32)
                + self.piece1[0, i].astype(F32)
                + self.piece1[1, i].astype(F32)
            )
            mine[i] = total.astype(BF16)

        self.sent = [
            self.copies.start(
                mine.at[lax.rem(self.at[self.second] + step, 4)],
                self.piece2.at[step - 1],
                moved(self.at, self.second, step),
            )
            for step in (1, 2, 3)
        ]

    def finish(self):
        total = self.pair[self.slot(0), self.at[self.second]].astype(F32)
        for copy in self.sent:
            copy.wait()
        for i in range(3):
            total = total + self.piece2[i].astype(F32)
        return total


def part_scratch(rows, columns):
    return [
        pltpu.VMEM((2, 4, 4, rows, columns), BF16),
        pltpu.VMEM((4, 4, rows, columns), BF16),
        pltpu.VMEM((2, 2, rows, columns), BF16),
        pltpu.VMEM((2, 4, rows, columns), BF16),
        pltpu.VMEM((3, rows, columns), BF16),
    ]


def line_send(at, copies, lines, line_in):
    return [
        copies.start(
            lines.at[lax.rem(at["x"] + step, 4)], line_in.at[step - 1], moved(at, "x", step)
        )
        for step in (1, 2, 3)
    ]


def line_finish(at, started, lines, line_in):
    total = lines[at["x"]].astype(F32)
    for copy in started:
        copy.wait()
    for i in range(3):
        total = total + line_in[i].astype(F32)
    return total


def line_scratch(rows):
    return [pltpu.VMEM((4, rows, D), BF16), pltpu.VMEM((3, rows, D), BF16)]


def share_all(at, copies, axis, held, slots):
    size = 2 if axis == "c" else 4
    slots[at[axis]] = held[...]
    return [
        copies.start(held, slots.at[at[axis]], moved(at, axis, step)) for step in range(1, size)
    ]


def sum_shared(started, held, slots):
    for copy in started:
        copy.wait()
    total = slots[0]
    for i in range(1, slots.shape[0]):
        total = total + slots[i]
    held[...] = total


def shift_in_start(copies, source, rows_in, edge, edge_in):
    started = [copies.start(source.at[4:8], rows_in, neighbour(1, 0))]
    for half in range(2):
        ends = [source[4 * half + r, 32:48].astype(F32)[12:16] for r in range(4)]
        edge[half] = jnp.concatenate(ends, axis=0).astype(BF16)
    started.append(copies.start(edge.at[0], edge_in.at[0], neighbour(0, 1)))
    started.append(copies.start(edge.at[1], edge_in.at[1], neighbour(1, 1)))
    return started


def shift_in_finish(started, source, rows_in, edge_in, grid):
    for copy in started:
        copy.wait()
    for row in range(8):
        held = (rows_in[row] if row < 4 else source[row - 4]).astype(F32)
        turned = pltpu.roll(held, 4, 0)
        ends = edge_in[1 if row < 4 else 0].astype(F32)[4 * (row % 4) : 4 * (row % 4) + 4]
        grid[row] = jnp.concatenate(
            [jnp.concatenate([ends, turned[4:8]], axis=0), turned[8:48]], axis=0
        )


def shift_back_start(copies, grid, rows_out, rows_in, edge, edge_in):
    for row in range(4):
        rows_out[row] = pltpu.roll(grid[row], 44, 0).astype(BF16)
    started = [copies.start(rows_out, rows_in, neighbour(-1, 0))]
    for half in range(2):
        firsts = [grid[4 * half + r, 0:8][0:4] for r in range(4)]
        edge[half] = jnp.concatenate(firsts, axis=0).astype(BF16)
    started.append(copies.start(edge.at[1], edge_in.at[1], neighbour(0, -1)))
    started.append(copies.start(edge.at[0], edge_in.at[0], neighbour(-1, -1)))
    return started


def shift_back_finish(started, grid, rows_in, edge_in, result):
    for copy in started:
        copy.wait()
    for row in range(8):
        if row < 4:
            turned = pltpu.roll(grid[row + 4], 44, 0)
        else:
            turned = rows_in[row - 4].astype(F32)
        ends = edge_in[1 if row < 4 else 0].astype(F32)[4 * (row % 4) : 4 * (row % 4) + 4]
        whole = jnp.concatenate(
            [turned[0:40], jnp.concatenate([turned[40:44], ends], axis=0)], axis=0
        )
        result[row] = whole.astype(result.dtype)


SHIFT_SCRATCH = [
    pltpu.VMEM((4, 48, D), BF16),
    pltpu.VMEM((2, 16, D), BF16),
    pltpu.VMEM((2, 16, D), BF16),
]


TOKENS = 384
WINDOWS = 6
PAIRS = 4
TILE = 16


def mm(a, b):
    return lax.dot_general(a, b, (((1,), (0,)), ((), ())), preferred_element_type=F32)


def mm_nt(a, b):
    return lax.dot_general(a, b, (((1,), (1,)), ((), ())), preferred_element_type=F32)


def mm_tn(a, b):
    return lax.dot_general(a, b, (((0,), (0,)), ((), ())), preferred_element_type=F32)


def split_low(value):
    high = value.astype(BF16)
    return high, (value - high.astype(F32)).astype(BF16)


def iota(shape, dim):
    return lax.broadcasted_iota(jnp.int32, shape, dim)


def tiles(body):
    @pl.loop(0, TOKENS // TILE, unroll=8)
    def _(i):
        body(i, pl.ds(pl.multiple_of(i * TILE, TILE), TILE))


def grid_tile(grid, i):
    window, row = i // 4, lax.rem(i, 4) * 2
    columns = pl.ds(pl.multiple_of(window * 8, 8), 8)
    return jnp.concatenate([grid[row, columns], grid[row + 1, columns]], axis=0)


def store_grid_tile(grid, i, tile):
    window, row = i // 4, lax.rem(i, 4) * 2
    columns = pl.ds(pl.multiple_of(window * 8, 8), 8)
    grid[row, columns] = tile[0:8]
    grid[row + 1, columns] = tile[8:16]


def normalise(vectors):
    centred = vectors - jnp.mean(vectors, axis=-1, keepdims=True)
    factor = lax.rsqrt(jnp.mean(centred * centred, axis=-1, keepdims=True) + NORM_EPSILON)
    return centred * factor, factor


def normalise_back(grad_out, normal, factor, gain):
    grad_hat = grad_out * gain
    inner = (
        grad_hat
        - jnp.mean(grad_hat, axis=-1, keepdims=True)
        - normal * jnp.mean(grad_hat * normal, axis=-1, keepdims=True)
    )
    return factor * inner


def line_order(first_z):
    place_of = iota((1, D), 1)
    core, first, second = place_of >> 8, (place_of >> 6) & 3, (place_of >> 4) & 3
    x, r = (place_of >> 2) & 3, place_of & 3
    y, z = (second, first) if first_z else (first, second)
    feature = (y << 7) | ((z & 1) << 6) | ((z >> 1) << 5) | (x << 3) | (core << 2) | r
    return jnp.where(iota((D, D), 0) == feature, 1.0, 0.0).astype(BF16)


def pair_offsets():
    row, column = iota((256, 128), 0), iota((256, 128), 1)
    target = ((column >> 6) << 7) + 15 * ((column >> 3) & 7) + (column & 7)
    return jnp.where(row == target, 1.0, 0.0).astype(BF16)


def store_wide(halves, i, rows):
    halves[0, 8 * i : 8 * i + 8] = rows[:, 0:128]
    halves[1, 8 * i : 8 * i + 8] = rows[:, 128:256]


def load_strided(halves, first):
    return jnp.concatenate([halves[k, pl.ds(first, 8, stride=8), :] for k in range(2)], axis=1)


def expand_bias(rel, table, shifted, bias, masked):
    table[...] = jnp.zeros_like(table)
    table[:, 0:225] = rel[...]
    whole = table[...]
    for b in range(8):
        store_wide(shifted, b, pltpu.roll(whole, (256 - (7 - b)) % 256, 1))
    spread = pair_offsets()
    key, query = iota((64, 128), 0), iota((64, 128), 1) & 63
    apart = jnp.where((key >> 5) == (query >> 5), 0.0, -1e30)
    apart = jnp.where(masked, apart, 0.0)
    for p in range(PAIRS):
        heads = []
        for h in (2 * p, 2 * p + 1):
            rows = load_strided(shifted, h)
            turned = [pltpu.roll(rows, 256 - (105 - 15 * a), 1)[:, 0:128] for a in range(8)]
            heads.append(jnp.concatenate(turned, axis=0))
        high, low = split_low(jnp.concatenate(heads, axis=1))
        bias[p] = mm(high, spread) + mm(low, spread) + apart


def collect_table(grad_bias, collected, total):
    spread = pair_offsets()
    for p in range(PAIRS):
        high, low = split_low(grad_bias[p])
        both = mm_nt(high, spread) + mm_nt(low, spread)
        for k in range(2):
            one = both[:, 128 * k : 128 * k + 128]
            one = jnp.concatenate([one, jnp.zeros_like(one)], axis=1)
            rows = one[56:64]
            for a in range(7):
                rows = rows + pltpu.roll(one[8 * a : 8 * a + 8], 105 - 15 * a, 1)
            h = 2 * p + k
            store_wide(collected, h, rows)
    table = load_strided(collected, 7)
    for b in range(7):
        table = table + pltpu.roll(load_strided(collected, b), 7 - b, 1)
    total[...] = table


def both_heads(pair):
    left = iota(pair.shape, 1) < 64
    zero = jnp.zeros_like(pair)
    return jnp.concatenate([jnp.where(left, pair, zero), jnp.where(left, zero, pair)], axis=0)


def own_heads(crossed):
    return jnp.where(iota((64, 128), 1) < 64, crossed[0:64], crossed[64:128])


def window_rows(w):
    return pl.ds(pl.multiple_of(w * 64, 64), 64)


def attend(w, qkv, bias, probs, attended):
    rows = window_rows(w)
    for p in range(PAIRS):
        query = qkv[rows, 128 * p : 128 * p + 128]
        keys = qkv[rows, D + 128 * p : D + 128 * p + 128]
        values = qkv[rows, 2 * D + 128 * p : 2 * D + 128 * p + 128]
        scores = mm_nt(keys, both_heads(query)) + bias[p]
        powers = jnp.exp(scores - jnp.max(scores, axis=0, keepdims=True))
        each = powers / jnp.sum(powers, axis=0, keepdims=True)
        probs[w, p] = each
        crossed = mm_tn(each.astype(BF16), values)
        attended[rows, 128 * p : 128 * p + 128] = own_heads(crossed).astype(BF16)


def attend_back(w, qkv, probs, grad_attended, grad_bias, grad_rows):
    rows = window_rows(w)
    for p in range(PAIRS):
        query = both_heads(qkv[rows, 128 * p : 128 * p + 128])
        keys = qkv[rows, D + 128 * p : D + 128 * p + 128]
        values = qkv[rows, 2 * D + 128 * p : 2 * D + 128 * p + 128]
        grads = both_heads(grad_attended[rows, 128 * p : 128 * p + 128])
        each = probs[w, p]
        grad_probs = mm_nt(values, grads)
        grad_scores = each * (grad_probs - jnp.sum(each * grad_probs, axis=0, keepdims=True))
        grad_bias[p] += grad_scores
        low = grad_scores.astype(BF16)
        grad_query = own_heads(mm_tn(low, keys)) * 0.125
        grad_rows[rows, 128 * p : 128 * p + 128] = grad_query.astype(BF16)
        grad_rows[rows, D + 128 * p : D + 128 * p + 128] = mm(low, query).astype(BF16)
        grad_rows[rows, 2 * D + 128 * p : 2 * D + 128 * p + 128] = mm(
            each.astype(BF16), grads
        ).astype(BF16)


GELU_SCALE = 0.7978845608028654
GELU_CUBE = 0.044715


def gelu_both(hidden):
    square = hidden * hidden
    swing = jnp.tanh(GELU_SCALE * hidden * (1.0 + GELU_CUBE * square))
    half = 0.5 + 0.5 * swing
    slope = half + (0.5 * GELU_SCALE) * hidden * (1.0 - swing * swing) * (
        1.0 + 3.0 * GELU_CUBE * square
    )
    return hidden * half, slope


def eight(tile):
    return tile[0:8] + tile[8:16]


COMPUTE_SCRATCH = [
    ("hat1", (TOKENS, D), F32),
    ("factor1", (TOKENS, 128), F32),
    ("norm1", (TOKENS, D), BF16),
    ("qkv", (TOKENS, 3 * D), BF16),
    ("attended", (TOKENS, D), BF16),
    ("resid", (TOKENS, D), F32),
    ("hat2", (TOKENS, D), F32),
    ("factor2", (TOKENS, 128), F32),
    ("norm2", (TOKENS, D), BF16),
    ("norm2_z", (TOKENS, D), BF16),
    ("cot", (TOKENS, D), BF16),
    ("hidden", (TOKENS, D), F32),
    ("grad_active", (TOKENS, D), F32),
    ("active", (TOKENS, D), BF16),
    ("grad_hidden", (TOKENS, D), BF16),
    ("mlp_out", (TOKENS, D), F32),
    ("grad_norm", (TOKENS, D), F32),
    ("grad_resid", (TOKENS, D), F32),
    ("grad_resid_low", (TOKENS, D), BF16),
    ("grad_attended", (TOKENS, D), BF16),
    ("grad_rows", (TOKENS, 3 * D), BF16),
    ("probs", (WINDOWS, PAIRS, 64, 128), F32),
    ("bias", (PAIRS, 64, 128), F32),
    ("grad_bias", (PAIRS, 64, 128), F32),
    ("table", (8, 256), F32),
    ("shifted", (2, 64, 128), F32),
    ("gain_sums", (2, 8, D), F32),
]


class Block:
    def __init__(self, refs):
        for (name, _, _), ref in zip(COMPUTE_SCRATCH, refs):
            setattr(self, name, ref)


def attention_forward(s, x_grid, gain_attn, w_qkv):
    def first_norm(i, rows):
        normal, factor = normalise(grid_tile(x_grid, i))
        s.hat1[rows] = normal
        s.factor1[rows] = jnp.broadcast_to(factor, (TILE, 128))
        s.norm1[rows] = (normal * gain_attn[...]).astype(BF16)

    tiles(first_norm)
    for i in range(3):
        columns = slice(D * i, D * i + D)
        part = mm(s.norm1[...], w_qkv[:, columns])
        s.qkv[:, columns] = (part * 0.125 if i == 0 else part).astype(BF16)

    @pl.loop(0, WINDOWS, unroll=3)
    def _(w):
        attend(w, s.qkv, s.bias, s.probs, s.attended)


def before_mlp(s, x_grid, c_grid, gain_mlp):
    def second_norm(i, rows):
        resid = s.resid[rows] + grid_tile(x_grid, i)
        normal, factor = normalise(resid)
        s.resid[rows] = resid
        s.hat2[rows] = normal
        s.factor2[rows] = jnp.broadcast_to(factor, (TILE, 128))
        s.norm2[rows] = (normal * gain_mlp[...]).astype(BF16)
        s.cot[rows] = grid_tile(c_grid, i).astype(BF16)

    tiles(second_norm)
    s.norm2_z[...] = mm(s.norm2[...], line_order(True)).astype(BF16)
    s.mlp_out[...] = jnp.zeros_like(s.mlp_out)
    s.grad_norm[...] = jnp.zeros_like(s.grad_norm)


def mlp_step(s, j, w_fc1, w_fc2, own_fc2, own_fc1):
    columns = pl.ds(pl.multiple_of(j * D, D), D)
    s.hidden[...] = mm(s.norm2[...], w_fc1[:, columns])
    s.grad_active[...] = mm_nt(s.cot[...], w_fc2[columns])

    def bend(_, rows):
        active, slope = gelu_both(s.hidden[rows])
        s.active[rows] = active.astype(BF16)
        s.grad_hidden[rows] = (slope * s.grad_active[rows]).astype(BF16)

    tiles(bend)
    grad_fc2 = mm_tn(s.active[...], s.cot[...]).astype(BF16).reshape(2, 2, 4, 2, 16, D)
    for low in range(2):
        for high in range(2):
            for x in range(4):
                for c in range(2):
                    own_fc2[c, j, 2 * high + low, 16 * x : 16 * x + 16, :] = grad_fc2[
                        low, high, x, c
                    ]
    grad_fc1 = mm_tn(s.norm2_z[...], s.grad_hidden[...]).astype(BF16)
    own_fc1[:, :, :, pl.ds(pl.multiple_of(j * 16, 16), 16), :] = grad_fc1.reshape(2, 4, 4, 16, D)
    s.mlp_out[...] += mm(s.active[...], w_fc2[columns])
    s.grad_norm[...] += mm_nt(s.grad_hidden[...], w_fc1[:, columns])


def after_mlp(s, gain_mlp, out_grid):
    s.gain_sums[...] = jnp.zeros_like(s.gain_sums)

    def second_back(i, rows):
        grad, normal = s.grad_norm[rows], s.hat2[rows]
        s.gain_sums[1] += eight(grad * normal)
        grad_resid = s.cot[rows].astype(F32) + normalise_back(
            grad, normal, s.factor2[rows][:, 0:1], gain_mlp[...]
        )
        s.grad_resid[rows] = grad_resid
        s.grad_resid_low[rows] = grad_resid.astype(BF16)
        store_grid_tile(out_grid, i, s.resid[rows] + s.mlp_out[rows])

    tiles(second_back)


def attention_after(s, gain_attn, grad_grid, small):
    def first_back(i, rows):
        grad, normal = s.grad_norm[rows], s.hat1[rows]
        s.gain_sums[0] += eight(grad * normal)
        back = normalise_back(grad, normal, s.factor1[rows][:, 0:1], gain_attn[...])
        store_grid_tile(grad_grid, i, s.grad_resid[rows] + back)

    tiles(first_back)
    collect_table(s.grad_bias, s.shifted, s.table)
    small[...] = jnp.zeros_like(small)
    small[0, 0:1] = jnp.sum(s.gain_sums[0], axis=0, keepdims=True)
    small[0, 1:2] = jnp.sum(s.gain_sums[1], axis=0, keepdims=True)
    small[1, :, 0:256] = s.table[...]


def whole_kernel(
    tokens, cotangent, gain_attn, rel, gain_mlp, w_qkv_hbm, w_proj_hbm, w_fc1_hbm, w_fc2_hbm,
    output, grad_tokens, qkv_total, fc1_total, fc2_total, small_total, *scratch
):
    refs = list(scratch)

    def take(count):
        taken = refs[:count]
        del refs[:count]
        return taken

    s = Block(take(len(COMPUTE_SCRATCH)))
    weights, weight_sem = take(4), take(1)[0]
    w_qkv, w_proj, w_fc1, w_fc2 = weights
    x_grid, c_grid, out_grid, grad_grid, small = take(5)
    send_sems, recv_sems = take(2)
    at = place()
    copies = Copies(send_sems, recv_sems)
    fc2 = Part(at, copies, ("y", "z"), *take(5))
    fc1 = Part(at, copies, ("z", "y"), *take(5))
    qkv_y = Part(at, copies, ("y", "z"), *take(5))
    qkv_z = Part(at, copies, ("z", "y"), *take(5))
    fc2_lines, fc1_lines, qkv_lines = take(2), take(2), take(2)
    held, pair_slots, slots = take(3)
    in_tokens, in_cot = take(3), take(3)
    back_out, back_tokens = take(4), take(4)

    loads = []
    for i, source in enumerate((w_qkv_hbm, w_proj_hbm, w_fc1_hbm, w_fc2_hbm)):
        loads.append(pltpu.make_async_copy(source, weights[i], weight_sem.at[i]))
        loads[-1].start()
    greet(at)
    came_tokens = shift_in_start(copies, tokens, *in_tokens)
    came_cot = shift_in_start(copies, cotangent, *in_cot)
    expand_bias(rel, s.table, s.shifted, s.bias, lax.axis_index("lat") == 0)
    shift_in_finish(came_tokens, tokens, in_tokens[0], in_tokens[2], x_grid)
    loads[0].wait()
    attention_forward(s, x_grid, gain_attn, w_qkv)
    for load in loads[1:]:
        load.wait()
    s.resid[...] = mm(s.attended[...], w_proj[...])
    shift_in_finish(came_cot, cotangent, in_cot[0], in_cot[2], c_grid)
    before_mlp(s, x_grid, c_grid, gain_mlp)

    @pl.loop(0, 4)
    def _(i):
        mlp_step(s, fc2.slot(6 - i), w_fc1, w_fc2, fc2.own, fc1.own)
        fc2.pair_copy(i).start()

    after_mlp(s, gain_mlp, out_grid)
    went_out = shift_back_start(copies, out_grid, *back_out)
    by_z = line_order(True)
    s.norm2_z[...] = mm(s.attended[...], by_z).astype(BF16)
    grad_proj = mm_tn(s.norm2_z[...], s.grad_resid_low[...]).astype(BF16)
    fc1.own[:, :, :, 64:80, :] = grad_proj.reshape(2, 4, 4, 16, D)
    fc1.begin()
    fc2.first_halves()
    s.grad_attended[...] = mm_nt(s.grad_resid_low[...], w_proj[...]).astype(BF16)
    s.grad_bias[...] = jnp.zeros_like(s.grad_bias)

    def windows_back(first, last):
        @pl.loop(first, last, unroll=2)
        def _(w):
            attend_back(w, s.qkv, s.probs, s.grad_attended, s.grad_bias, s.grad_rows)

    windows_back(0, 2)
    fc2.first_pieces()
    fc1.first_halves()
    windows_back(2, 4)
    fc1.first_pieces()
    windows_back(4, 6)
    s.norm2_z[...] = mm(s.norm1[...], by_z).astype(BF16)
    s.norm2[...] = mm(s.norm1[...], line_order(False)).astype(BF16)
    for i in range(3):
        for left, turned, part in ((0, s.norm2, qkv_y), (256, s.norm2_z, qkv_z)):
            columns = slice(D * i + left, D * i + left + 256)
            grad = mm_tn(turned[...], s.grad_rows[:, columns]).astype(BF16)
            part.own[:, :, :, 16 * i : 16 * i + 16, :] = grad.reshape(2, 4, 4, 16, 256)
    qkv_y.begin()
    qkv_z.begin()
    fc2.second_send()
    s.grad_norm[...] = mm_nt(s.grad_rows[...], w_qkv[...])
    qkv_y.first_halves()
    qkv_z.first_halves()
    fc1.second_send()
    attention_after(s, gain_attn, grad_grid, small)
    went_tokens = shift_back_start(copies, grad_grid, *back_tokens)
    held[0] = small[...]
    shared = share_all(at, copies, "c", held.at[0], pair_slots)
    qkv_y.first_pieces()
    qkv_z.first_pieces()
    sum_shared(shared, held.at[1], pair_slots)
    shared = share_all(at, copies, "y", held.at[1], slots.at[0])
    fc2_lines[0][...] = fc2.finish().astype(BF16).reshape(4, 16, D)
    fc2_sent = line_send(at, copies, *fc2_lines)
    total = fc1.finish()
    for x in range(4):
        rows = [total[16 * i + 4 * x : 16 * i + 4 * x + 4] for i in range(5)]
        fc1_lines[0][x] = jnp.concatenate(rows + [jnp.zeros((12, D), F32)], axis=0).astype(BF16)
    fc1_sent = line_send(at, copies, *fc1_lines)
    qkv_y.second_send()
    qkv_z.second_send()
    sum_shared(shared, held.at[2], slots.at[0])
    shared = share_all(at, copies, "z", held.at[2], slots.at[1])
    shift_back_finish(went_out, out_grid, back_out[1], back_out[3], output)
    total = jnp.concatenate([qkv_y.finish(), qkv_z.finish()], axis=1)
    for x in range(4):
        rows = [total[16 * i + 4 * x : 16 * i + 4 * x + 4] for i in range(3)]
        qkv_lines[0][x] = jnp.concatenate(rows + [jnp.zeros((4, D), F32)], axis=0).astype(BF16)
    qkv_sent = line_send(at, copies, *qkv_lines)
    sum_shared(shared, held.at[3], slots.at[1])
    shared = share_all(at, copies, "x", held.at[3], slots.at[2])
    shift_back_finish(went_tokens, grad_grid, back_tokens[1], back_tokens[3], grad_tokens)
    fc2_total[...] = line_finish(at, fc2_sent, *fc2_lines)
    fc1_total[...] = line_finish(at, fc1_sent, *fc1_lines)
    qkv_total[...] = line_finish(at, qkv_sent, *qkv_lines)
    sum_shared(shared, small_total, slots.at[2])


def whole(tokens, cotangent, gain_attn, w_qkv, w_proj, rel, gain_mlp, w_fc1, w_fc2):
    vmem = pl.BlockSpec(memory_space=pltpu.VMEM)
    copies = 100
    return pl.pallas_call(
        whole_kernel,
        out_shape=(
            jax.ShapeDtypeStruct((8, 48, D), BF16),
            jax.ShapeDtypeStruct((8, 48, D), F32),
            jax.ShapeDtypeStruct((16, D), F32),
            jax.ShapeDtypeStruct((32, D), F32),
            jax.ShapeDtypeStruct((16, D), F32),
            jax.ShapeDtypeStruct((2, 8, D), F32),
        ),
        in_specs=[vmem] * 5 + [pl.BlockSpec(memory_space=pl.ANY)] * 4,
        out_specs=[vmem] * 6,
        scratch_shapes=[pltpu.VMEM(shape, kind) for _, shape, kind in COMPUTE_SCRATCH]
        + [pltpu.VMEM(w.shape, BF16) for w in (w_qkv, w_proj, w_fc1, w_fc2)]
        + [pltpu.SemaphoreType.DMA((4,))]
        + [pltpu.VMEM((8, 48, D), F32)] * 4
        + [pltpu.VMEM((2, 8, D), F32)]
        + [pltpu.SemaphoreType.DMA((copies,))] * 2
        + part_scratch(64, D)
        + part_scratch(80, D)
        + part_scratch(48, 256) * 2
        + line_scratch(16)
        + line_scratch(32)
        + line_scratch(16)
        + [
            pltpu.VMEM((4, 2, 8, D), F32),
            pltpu.VMEM((2, 2, 8, D), F32),
            pltpu.VMEM((3, 4, 2, 8, D), F32),
        ]
        + SHIFT_SCRATCH * 2
        + ([pltpu.VMEM((4, 48, D), BF16)] + SHIFT_SCRATCH) * 2,
        compiler_params=pltpu.CompilerParams(
            collective_id=0, has_side_effects=True, vmem_limit_bytes=56 * 2**20
        ),
        name="whole_block",
    )(tokens, cotangent, gain_attn.reshape(1, D), rel, gain_mlp.reshape(1, D), w_qkv, w_proj, w_fc1, w_fc2)


def deliver_kernel(
    output, grad_tokens, qkv_total, fc1_total, fc2_total, small,
    output_to, grad_tokens_to, grad_qkv, grad_proj, table, grad_fc1, grad_fc2, gain_attn, gain_mlp,
    sems
):
    first = pltpu.make_async_copy(grad_tokens, grad_tokens_to, sems.at[0])
    second = pltpu.make_async_copy(output, output_to, sems.at[1])
    first.start()
    second.start()
    for i in range(3):
        grad_qkv[:, D * i : D * i + D] = qkv_total[4 * i : 4 * i + 4]
    for i in range(4):
        grad_fc1[:, D * i : D * i + D] = fc1_total[4 * i : 4 * i + 4]
    grad_proj[...] = fc1_total[16:20]
    grad_fc2[...] = fc2_total[...]
    table[...] = small[1][:, 0:225]
    gain_attn[...] = small[0, 0]
    gain_mlp[...] = small[0, 1]
    first.wait()
    second.wait()


def deliver(*results):
    vmem, anywhere = pl.BlockSpec(memory_space=pltpu.VMEM), pl.BlockSpec(memory_space=pl.ANY)
    return pl.pallas_call(
        deliver_kernel,
        out_shape=(
            jax.ShapeDtypeStruct((8, 48, D), BF16),
            jax.ShapeDtypeStruct((8, 48, D), F32),
            jax.ShapeDtypeStruct((4, 3 * D), F32),
            jax.ShapeDtypeStruct((4, D), F32),
            jax.ShapeDtypeStruct((8, 225), F32),
            jax.ShapeDtypeStruct((4, 4 * D), F32),
            jax.ShapeDtypeStruct((16, D), F32),
            jax.ShapeDtypeStruct((D,), F32),
            jax.ShapeDtypeStruct((D,), F32),
        ),
        in_specs=[anywhere] * 2 + [vmem] * 4,
        out_specs=[anywhere] * 2 + [vmem] * 7,
        scratch_shapes=[pltpu.SemaphoreType.DMA((2,))],
        name="deliver",
    )(*results)


def shards(tokens, cotangent, gain_attn, w_qkv, w_proj, rel_table, gain_mlp, w_fc1, w_fc2):
    return deliver(
        *whole(tokens, cotangent, gain_attn, w_qkv, w_proj, rel_table, gain_mlp, w_fc1, w_fc2)
    )


def solution(mesh):
    placed = (P("lat", "lon", None), P("lat", "lon", None), P(), P(), P(), P(), P(), P(), P())
    return jax.shard_map(
        shards,
        mesh=mesh,
        in_specs=placed,
        out_specs=(
            P("lat", "lon", None),
            P("lat", "lon", None),
            P(("lat", "lon"), None),
            P(("lat", "lon"), None),
            P(),
            P(("lat", "lon"), None),
            P(("lat", "lon"), None),
            P(),
            P(),
        ),
        check_vma=False,
    )
```

time: 124 us -> 122 us (0.984)
  local copies, waits for them, and re-layouts: 8.96 us -> 0 us
  Pallas kernels: 114 us -> 121 us
    pallas_call x3 -> x2, Pallas kernels: 114 us -> 121 us  [the longest x1 82.7 us: whole(): pl.pallas_call(whole_kernel, out_shape=(jax.ShapeDtypeStruct((8, 48, D),...]
    unnamed x14 -> x0, local copies, waits for them, and re-layouts: 6.28 us -> none
    slice x1 -> x0, local copies, waits for them, and re-layouts: 1.38 us -> none  [shards(): small[0, 1]]
    squeeze x1 -> x0, local copies, waits for them, and re-layouts: 1.3 us -> none  [shards(): small[1, :, :225]]
where the time goes in v1:
time: 122 us
  Pallas kernels  121 us (99%)
    pallas_call x1, Pallas kernels, whole(): pl.pallas_call(whole_kernel, out_shape=(jax.ShapeDtypeStruct((8, 48, D),...  82.7 us
    pallas_call x1, Pallas kernels, deliver(): pl.pallas_call(deliver_kernel, out_shape=(jax.ShapeDtypeStruct((8, 48, D)...  38.3 us

profile of v1, /device:TPU:0, one launch (start us, length us, event | category | flops | bytes accessed | tf_op | source)
XLA Modules:
  0.0 121.7 jit_solution(17081789792268781164)
XLA Ops:
  0.6 82.7 %whole_block.1 = (bf16[8,48,512]{2,1,0:T(8,128)(2,1)}, f32[8,48,512]{2,1,0:T(8,128)}, f32[16,512]{1,0:T(8,128)}, f32[32,512]{1,0:T(8,128)}, f32[16,512]{1,0:T(8,128)}, /*index=5*/f32[2,8,512]{2,1,0:T(8,128)}) custom-call(bf16[8,48,512]{2,1,0:T(8,128)(2,1)} %tokens.1, bf16[8,48,512]{2,1,0:T(8,128)(2,1)} %cotangent.1, f32[1,512]{1,0:T(1,128)} %bitcast.2, ...), custom_call_target="tpu_custom_call" | custom-call | tf_op jit(solution)/shard_map/whole_block/pallas_call | solution.py:713
  83.3 38.3 %deliver.1 = (bf16[8,48,512]{2,1,0:T(8,128)(2,1)}, f32[8,48,512]{2,1,0:T(8,128)}, f32[4,1536]{1,0:T(4,128)}, f32[4,512]{1,0:T(4,128)}, f32[8,225]{1,0:T(8,128)},...) custom-call(bf16[8,48,512]{2,1,0:T(8,128)(2,1)} %get-tuple-element.15.output, ...), custom_call_target="tpu_custom_call" | custom-call | tf_op jit(solution)/shard_map/deliver/pallas_call | solution.py:775

commit v2 on v1

--- a/solution.py
+++ b/solution.py
@@ -79,7 +79,7 @@
 def add_into(target, other, count):
     @pl.loop(0, count)
     def _(i):
-        target[i] = (target[i].astype(F32) + other[i].astype(F32)).astype(BF16)
+        target[i] = target[i] + other[i]
 
 
 class Part:
@@ -621,9 +621,9 @@
         loads[-1].start()
     greet(at)
     came_tokens = shift_in_start(copies, tokens, *in_tokens)
-    came_cot = shift_in_start(copies, cotangent, *in_cot)
     expand_bias(rel, s.table, s.shifted, s.bias, lax.axis_index("lat") == 0)
     shift_in_finish(came_tokens, tokens, in_tokens[0], in_tokens[2], x_grid)
+    came_cot = shift_in_start(copies, cotangent, *in_cot)
     loads[0].wait()
     attention_forward(s, x_grid, gain_attn, w_qkv)
     for load in loads[1:]:
@@ -750,13 +750,10 @@
 
 def deliver_kernel(
     output, grad_tokens, qkv_total, fc1_total, fc2_total, small,
-    output_to, grad_tokens_to, grad_qkv, grad_proj, table, grad_fc1, grad_fc2, gain_attn, gain_mlp,
-    sems
+    output_to, grad_tokens_to, grad_qkv, grad_proj, table, grad_fc1, grad_fc2, gain_attn, gain_mlp
 ):
-    first = pltpu.make_async_copy(grad_tokens, grad_tokens_to, sems.at[0])
-    second = pltpu.make_async_copy(output, output_to, sems.at[1])
-    first.start()
-    second.start()
+    grad_tokens_to[...] = grad_tokens[...]
+    output_to[...] = output[...]
     for i in range(3):
         grad_qkv[:, D * i : D * i + D] = qkv_total[4 * i : 4 * i + 4]
     for i in range(4):
@@ -766,12 +763,10 @@
     table[...] = small[1][:, 0:225]
     gain_attn[...] = small[0, 0]
     gain_mlp[...] = small[0, 1]
-    first.wait()
-    second.wait()
 
 
 def deliver(*results):
-    vmem, anywhere = pl.BlockSpec(memory_space=pltpu.VMEM), pl.BlockSpec(memory_space=pl.ANY)
+    vmem = pl.BlockSpec(memory_space=pltpu.VMEM)
     return pl.pallas_call(
         deliver_kernel,
         out_shape=(
@@ -785,9 +780,8 @@
             jax.ShapeDtypeStruct((D,), F32),
             jax.ShapeDtypeStruct((D,), F32),
         ),
-        in_specs=[anywhere] * 2 + [vmem] * 4,
-        out_specs=[anywhere] * 2 + [vmem] * 7,
-        scratch_shapes=[pltpu.SemaphoreType.DMA((2,))],
+        in_specs=[vmem] * 6,
+        out_specs=[vmem] * 9,
         name="deliver",
     )(*results)
 

time: 122 us -> 84.7 us (0.69)
  Pallas kernels: 121 us -> 83.9 us
    pallas_call x1, Pallas kernels: 38.3 us -> 2.35 us  [deliver(): pl.pallas_call(deliver_kernel, out_shape=(jax.ShapeDtypeStruct((8, 48, D)...]
where the time goes in v2:
time: 84.7 us; the launch traced here: 84.6 us
  Pallas kernels  83.9 us (99%)
    pallas_call x1, Pallas kernels, whole(): pl.pallas_call(whole_kernel, out_shape=(jax.ShapeDtypeStruct((8, 48, D),...  81.6 us
    pallas_call x1, Pallas kernels, deliver(): pl.pallas_call(deliver_kernel, out_shape=(jax.ShapeDtypeStruct((8, 48, D)...  2.35 us

profile of v2, /device:TPU:0, one launch (start us, length us, event | category | flops | bytes accessed | tf_op | source)
XLA Modules:
  0.0 84.6 jit_solution(13984910376110900470)
XLA Ops:
  0.6 81.6 %whole_block.1 = (bf16[8,48,512]{2,1,0:T(8,128)(2,1)}, f32[8,48,512]{2,1,0:T(8,128)}, f32[16,512]{1,0:T(8,128)}, f32[32,512]{1,0:T(8,128)}, f32[16,512]{1,0:T(8,128)}, /*index=5*/f32[2,8,512]{2,1,0:T(8,128)}) custom-call(bf16[8,48,512]{2,1,0:T(8,128)(2,1)} %tokens.1, bf16[8,48,512]{2,1,0:T(8,128)(2,1)} %cotangent.1, f32[1,512]{1,0:T(1,128)} %bitcast.2, ...), custom_call_target="tpu_custom_call" | custom-call | tf_op jit(solution)/shard_map/whole_block/pallas_call | solution.py:713
  82.2 2.4 %deliver.1 = (bf16[8,48,512]{2,1,0:T(8,128)(2,1)}, f32[8,48,512]{2,1,0:T(8,128)}, f32[4,1536]{1,0:T(4,128)}, f32[4,512]{1,0:T(4,128)}, f32[8,225]{1,0:T(8,128)},...) custom-call(bf16[8,48,512]{2,1,0:T(8,128)(2,1)} %get-tuple-element.15.output, ...), custom_call_target="tpu_custom_call" | custom-call | tf_op jit(solution)/shard_map/deliver/pallas_call | solution.py:770

commit v3 on v2

--- a/solution.py
+++ b/solution.py
@@ -25,10 +25,10 @@
     }
 
 
-def moved(at, axis, step):
-    size = 2 if axis == "c" else 4
+def moved(at, *hops):
     there = dict(at)
-    there[axis] = lax.rem(at[axis] + step, size)
+    for axis, step in hops:
+        there[axis] = lax.rem(at[axis] + step, 2 if axis == "c" else 4)
     lat = there["y"] * 2 + lax.rem(there["z"], 2)
     lon = (there["z"] // 2) * 8 + there["x"] * 2 + there["c"]
     return (lat, lon)
@@ -41,15 +41,19 @@
     )
 
 
+PLANE = [(i, j) for i in range(4) for j in range(4) if (i, j) != (0, 0)]
+
+
 def greet(at):
     barrier = pltpu.get_barrier_semaphore()
-    others = [moved(at, "c", 1)]
-    others += [moved(at, axis, step) for axis in ("y", "z", "x") for step in (1, 2, 3)]
+    others = [moved(at, ("c", 1))]
+    others += [moved(at, ("z", i), ("x", j)) for i, j in PLANE]
+    others += [moved(at, ("y", i), ("x", j)) for i, j in PLANE if i]
     steps = ((1, 0), (0, 1), (1, 1), (-1, 0), (0, -1), (-1, -1))
     others += [neighbour(*step) for step in steps]
     for other in others:
         pl.semaphore_signal(barrier, inc=1, device_id=other, device_id_type=MESH)
-    pl.semaphore_wait(barrier, len(others))
+    return len(others)
 
 
 class Copies:
@@ -76,84 +80,80 @@
         return copy
 
 
-def add_into(target, other, count):
-    @pl.loop(0, count)
-    def _(i):
-        target[i] = target[i] + other[i]
-
-
 class Part:
-    def __init__(self, at, copies, axes, own, pair, half1, piece1, piece2):
+    def __init__(self, at, copies, axes, own, pair, piece1, piece2):
         self.at, self.copies = at, copies
         self.first, self.second = axes
-        self.own, self.pair = own, pair
-        self.half1, self.piece1, self.piece2 = half1, piece1, piece2
-        self.base = copies.reserve(4)
+        self.own, self.pair, self.piece1, self.piece2 = own, pair, piece1, piece2
+        self.pairs, self.sent = {}, []
 
     def slot(self, step):
         return lax.rem(self.at[self.first] + step, 4)
 
-    def pair_copy(self, i):
-        j = self.slot(6 - i)
-        return self.copies.make(
-            self.base + i, self.own.at[1 - self.at["c"], j], self.pair.at[j], moved(self.at, "c", 1)
+    def place_start(self, step):
+        j = self.slot(step)
+        self.pairs[step] = self.copies.start(
+            self.own.at[1 - self.at["c"], j], self.pair.at[j], moved(self.at, ("c", 1))
         )
 
-    def begin(self):
-        for i in range(4):
-            self.pair_copy(i).start()
-
-    def pair_sum(self, i):
-        self.pair_copy(i).wait()
-        j = self.slot(6 - i)
-        add_into(self.pair.at[j], self.own.at[self.at["c"], j], 4)
-
-    def first_halves(self):
-        self.pair_sum(0)
-        j = self.slot(2)
-        self.up = self.copies.start(
-            self.pair.at[j, 0:2], self.half1.at[0], moved(self.at, self.first, 1)
-        )
-        self.down = self.copies.start(
-            self.pair.at[j, 2:4], self.half1.at[1], moved(self.at, self.first, 3)
-        )
-        self.pair_sum(1)
-        self.pair_sum(3)
-
-    def first_pieces(self):
-        self.up.wait()
-        add_into(self.pair.at[self.slot(1), 0:2], self.half1.at[0], 2)
-        self.up = self.copies.start(
-            self.pair.at[self.slot(1)], self.piece1.at[0], moved(self.at, self.first, 1)
-        )
-        self.down.wait()
-        add_into(self.pair.at[self.slot(3), 2:4], self.half1.at[1], 2)
-        self.down = self.copies.start(
-            self.pair.at[self.slot(3)], self.piece1.at[1], moved(self.at, self.first, 3)
-        )
-        self.pair_sum(2)
-
-    def second_send(self):
-        self.up.wait()
-        self.down.wait()
-        mine = self.pair.at[self.slot(0)]
+    def place_send(self, step):
+        self.pairs[step].wait()
+        j, c = self.slot(step), self.at["c"]
 
         @pl.loop(0, 4)
         def _(i):
-            total = (
-                mine[i].astype(F32)
-                + self.piece1[0, i].astype(F32)
-                + self.piece1[1, i].astype(F32)
+            self.pair[j, i] = self.pair[j, i] + self.own[c, j, i]
+
+        if step:
+            self.sent.append(
+                self.copies.start(
+                    self.pair.at[j], self.piece1.at[step - 1], moved(self.at, (self.first, step))
+                )
             )
+
+    def rows_start(self, key, rows):
+        self.pairs[key] = self.copies.start(
+            self.own.at[1 - self.at["c"], :, :, rows],
+            self.pair.at[:, :, rows],
+            moved(self.at, ("c", 1)),
+        )
+
+    def rows_send(self, key, rows):
+        self.pairs[key].wait()
+        c = self.at["c"]
+
+        @pl.loop(0, 4)
+        def _(j):
+            self.pair[j, :, rows] = self.pair[j, :, rows] + self.own[c, j, :, rows]
+
+        for step in (2, 1, 3):
+            self.sent.append(
+                self.copies.start(
+                    self.pair.at[self.slot(step), :, rows],
+                    self.piece1.at[step - 1, :, rows],
+                    moved(self.at, (self.first, step)),
+                )
+            )
+
+    def second_send(self):
+        for copy in self.sent:
+            copy.wait()
+        mine = self.pair.at[self.slot(0)]
+
+        @pl.loop(0, 4)
+        def _(i):
+            total = mine[i].astype(F32)
+            for k in range(3):
+                total = total + self.piece1[k, i].astype(F32)
             mine[i] = total.astype(BF16)
 
         self.sent = [
             self.copies.start(
                 mine.at[lax.rem(self.at[self.second] + step, 4)],
                 self.piece2.at[step - 1],
-                moved(self.at, self.second, step),
+                moved(self.at, (self.second, step)),
             )
-            for step in (1, 2, 3)
+            for step in (2, 1, 3)
         ]
 
     def finish(self):
@@ -164,32 +164,61 @@
             total = total + self.piece2[i].astype(F32)
         return total
 
+    def plane_send(self, lines, lines_in):
+        for copy in self.sent:
+            copy.wait()
+        mine = self.slot(0)
+        for i in range(4):
+            total = self.pair[mine, i].astype(F32)
+            for k in range(3):
+                total = total + self.piece1[k, i].astype(F32)
+            for x in range(4):
+                rows = [total[16 * k + 4 * x : 16 * k + 4 * x + 4] for k in range(3)]
+                rows = rows + [jnp.zeros((4, total.shape[1]), F32)]
+                lines[i, x] = jnp.concatenate(rows, axis=0).astype(BF16)
+        at = self.at
+        self.sent = [
+            self.copies.start(
+                lines.at[lax.rem(at[self.second] + i, 4), lax.rem(at["x"] + j, 4)],
+                lines_in.at[4 * i + j - 1],
+                moved(at, (self.second, i), ("x", j)),
+            )
+            for i, j in PLANE
+        ]
+
+    def plane_finish(self, lines, lines_in):
+        total = lines[self.at[self.second], self.at["x"]].astype(F32)
+        for copy in self.sent:
+            copy.wait()
+        for i in range(15):
+            total = total + lines_in[i].astype(F32)
+        return total
+
 
 def part_scratch(rows, columns):
     return [
         pltpu.VMEM((2, 4, 4, rows, columns), BF16),
         pltpu.VMEM((4, 4, rows, columns), BF16),
-        pltpu.VMEM((2, 2, rows, columns), BF16),
-        pltpu.VMEM((2, 4, rows, columns), BF16),
+        pltpu.VMEM((3, 4, rows, columns), BF16),
         pltpu.VMEM((3, rows, columns), BF16),
     ]
 
 
-def line_send(at, copies, lines, line_in):
+def line_send(at, copies, axis, lines, lines_in):
     return [
         copies.start(
-            lines.at[lax.rem(at["x"] + step, 4)], line_in.at[step - 1], moved(at, "x", step)
+            lines.at[lax.rem(at[axis] + step, 4)], lines_in.at[step - 1], moved(at, (axis, step))
         )
-        for step in (1, 2, 3)
+        for step in (2, 1, 3)
     ]
 
 
-def line_finish(at, started, lines, line_in):
-    total = lines[at["x"]].astype(F32)
+def line_finish(at, started, axis, lines, lines_in):
+    total = lines[at[axis]].astype(F32)
     for copy in started:
         copy.wait()
     for i in range(3):
-        total = total + line_in[i].astype(F32)
+        total = total + lines_in[i].astype(F32)
     return total
 
 
@@ -197,12 +226,22 @@
     return [pltpu.VMEM((4, rows, D), BF16), pltpu.VMEM((3, rows, D), BF16)]
 
 
-def share_all(at, copies, axis, held, slots):
-    size = 2 if axis == "c" else 4
+def plane_scratch():
+    return [pltpu.VMEM((4, 4, 16, 256), BF16), pltpu.VMEM((15, 16, 256), BF16)]
+
+
+def share_line(at, copies, axis, held, slots):
     slots[at[axis]] = held[...]
     return [
-        copies.start(held, slots.at[at[axis]], moved(at, axis, step)) for step in range(1, size)
+        copies.start(held, slots.at[at[axis]], moved(at, (axis, step)))
+        for step in range(1, slots.shape[0])
     ]
+
+
+def share_plane(at, copies, held, slots):
+    mine = at["z"] * 4 + at["x"]
+    slots[mine] = held[...]
+    return [copies.start(held, slots.at[mine], moved(at, ("z", i), ("x", j))) for i, j in PLANE]
 
 
 def sum_shared(started, held, slots):
@@ -332,12 +371,12 @@
     return factor * inner
 
 
-def line_order(first_z):
+def line_order(axes):
     place_of = iota((1, D), 1)
-    core, first, second = place_of >> 8, (place_of >> 6) & 3, (place_of >> 4) & 3
-    x, r = (place_of >> 2) & 3, place_of & 3
-    y, z = (second, first) if first_z else (first, second)
-    feature = (y << 7) | ((z & 1) << 6) | ((z >> 1) << 5) | (x << 3) | (core << 2) | r
+    core, r = place_of >> 8, place_of & 3
+    at = {axis: (place_of >> shift) & 3 for axis, shift in zip(axes, (6, 4, 2))}
+    z = ((at["z"] & 1) << 6) | ((at["z"] >> 1) << 5)
+    feature = (at["y"] << 7) | z | (at["x"] << 3) | (core << 2) | r
     return jnp.where(iota((D, D), 0) == feature, 1.0, 0.0).astype(BF16)
 
 
@@ -471,7 +510,10 @@
     ("hat2", (TOKENS, D), F32),
     ("factor2", (TOKENS, 128), F32),
     ("norm2", (TOKENS, D), BF16),
-    ("norm2_z", (TOKENS, D), BF16),
+    ("turned", (TOKENS, D), BF16),
+    ("order_fc1", (D, D), BF16),
+    ("order_y", (D, D), BF16),
+    ("order_z", (D, D), BF16),
     ("cot", (TOKENS, D), BF16),
     ("hidden", (TOKENS, D), F32),
     ("grad_active", (TOKENS, D), F32),
@@ -527,12 +569,12 @@
         s.cot[rows] = grid_tile(c_grid, i).astype(BF16)
 
     tiles(second_norm)
-    s.norm2_z[...] = mm(s.norm2[...], line_order(True)).astype(BF16)
+    s.turned[...] = mm(s.norm2[...], s.order_fc1[...]).astype(BF16)
     s.mlp_out[...] = jnp.zeros_like(s.mlp_out)
     s.grad_norm[...] = jnp.zeros_like(s.grad_norm)
 
 
-def mlp_step(s, j, w_fc1, w_fc2, own_fc2, own_fc1):
+def mlp_step(s, j, block, w_fc1, w_fc2, own_fc2, own_fc1):
     columns = pl.ds(pl.multiple_of(j * D, D), D)
     s.hidden[...] = mm(s.norm2[...], w_fc1[:, columns])
     s.grad_active[...] = mm_nt(s.cot[...], w_fc2[columns])
@@ -551,8 +593,8 @@
                     own_fc2[c, j, 2 * high + low, 16 * x : 16 * x + 16, :] = grad_fc2[
                         low, high, x, c
                     ]
-    grad_fc1 = mm_tn(s.norm2_z[...], s.grad_hidden[...]).astype(BF16)
-    own_fc1[:, :, :, pl.ds(pl.multiple_of(j * 16, 16), 16), :] = grad_fc1.reshape(2, 4, 4, 16, D)
+    grad_fc1 = mm_tn(s.turned[...], s.grad_hidden[...]).astype(BF16)
+    own_fc1[:, :, :, block, :] = grad_fc1.reshape(2, 4, 4, 16, D)
     s.mlp_out[...] += mm(s.active[...], w_fc2[columns])
     s.grad_norm[...] += mm_nt(s.grad_hidden[...], w_fc1[:, columns])
 
@@ -581,11 +623,11 @@
         store_grid_tile(grad_grid, i, s.grad_resid[rows] + back)
 
     tiles(first_back)
-    collect_table(s.grad_bias, s.shifted, s.table)
-    small[...] = jnp.zeros_like(small)
-    small[0, 0:1] = jnp.sum(s.gain_sums[0], axis=0, keepdims=True)
-    small[0, 1:2] = jnp.sum(s.gain_sums[1], axis=0, keepdims=True)
-    small[1, :, 0:256] = s.table[...]
+    small[:, 256:512] = jnp.zeros((8, 256), F32)
+    for i in range(2):
+        total = jnp.sum(s.gain_sums[i], axis=0, keepdims=True)
+        small[2 * i : 2 * i + 1, 256:512] = total[:, 0:256]
+        small[2 * i + 1 : 2 * i + 2, 256:512] = total[:, 256:512]
 
 
 def whole_kernel(
@@ -606,12 +648,12 @@
     send_sems, recv_sems = take(2)
     at = place()
     copies = Copies(send_sems, recv_sems)
-    fc2 = Part(at, copies, ("y", "z"), *take(5))
-    fc1 = Part(at, copies, ("z", "y"), *take(5))
-    qkv_y = Part(at, copies, ("y", "z"), *take(5))
-    qkv_z = Part(at, copies, ("z", "y"), *take(5))
-    fc2_lines, fc1_lines, qkv_lines = take(2), take(2), take(2)
-    held, pair_slots, slots = take(3)
+    fc2 = Part(at, copies, ("y", "z"), *take(4))
+    fc1 = Part(at, copies, ("x", "z"), *take(4))
+    qkv_y = Part(at, copies, ("y", "z"), *take(4))
+    qkv_z = Part(at, copies, ("z", "y"), *take(4))
+    fc2_lines, fc1_lines, qkv_y_lines, qkv_z_lines = take(2), take(2), take(2), take(2)
+    held, pair_slots, y_slots, plane_slots = take(4)
     in_tokens, in_cot = take(3), take(3)
     back_out, back_tokens = take(4), take(4)
 
@@ -619,9 +661,13 @@
     for i, source in enumerate((w_qkv_hbm, w_proj_hbm, w_fc1_hbm, w_fc2_hbm)):
         loads.append(pltpu.make_async_copy(source, weights[i], weight_sem.at[i]))
         loads[-1].start()
-    greet(at)
+    partners = greet(at)
+    expand_bias(rel, s.table, s.shifted, s.bias, lax.axis_index("lat") == 0)
+    pl.semaphore_wait(pltpu.get_barrier_semaphore(), partners)
     came_tokens = shift_in_start(copies, tokens, *in_tokens)
-    expand_bias(rel, s.table, s.shifted, s.bias, lax.axis_index("lat") == 0)
+    s.order_fc1[...] = line_order(("x", "z", "y"))
+    s.order_y[...] = line_order(("y", "z", "x"))
+    s.order_z[...] = line_order(("z", "y", "x"))
     shift_in_finish(came_tokens, tokens, in_tokens[0], in_tokens[2], x_grid)
     came_cot = shift_in_start(copies, cotangent, *in_cot)
     loads[0].wait()
@@ -632,84 +678,74 @@
     shift_in_finish(came_cot, cotangent, in_cot[0], in_cot[2], c_grid)
     before_mlp(s, x_grid, c_grid, gain_mlp)
 
-    @pl.loop(0, 4)
-    def _(i):
-        mlp_step(s, fc2.slot(6 - i), w_fc1, w_fc2, fc2.own, fc1.own)
-        fc2.pair_copy(i).start()
-
+    steps = (2, 1, 3, 0)
+    blocks = [pl.ds(pl.multiple_of(16 * fc2.slot(step), 16), 16) for step in steps]
+    for i in range(4):
+        mlp_step(s, fc2.slot(steps[i]), blocks[i], w_fc1, w_fc2, fc2.own, fc1.own)
+        fc2.place_start(steps[i])
+        fc1.rows_start(i, blocks[i])
+        if i:
+            fc2.place_send(steps[i - 1])
+            fc1.rows_send(i - 1, blocks[i - 1])
     after_mlp(s, gain_mlp, out_grid)
+    fc1.rows_send(3, blocks[3])
+    fc2.place_send(0)
     went_out = shift_back_start(copies, out_grid, *back_out)
-    by_z = line_order(True)
-    s.norm2_z[...] = mm(s.attended[...], by_z).astype(BF16)
-    grad_proj = mm_tn(s.norm2_z[...], s.grad_resid_low[...]).astype(BF16)
+    s.turned[...] = mm(s.attended[...], s.order_fc1[...]).astype(BF16)
+    grad_proj = mm_tn(s.turned[...], s.grad_resid_low[...]).astype(BF16)
     fc1.own[:, :, :, 64:80, :] = grad_proj.reshape(2, 4, 4, 16, D)
-    fc1.begin()
-    fc2.first_halves()
+    fc1.rows_start(4, slice(64, 80))
     s.grad_attended[...] = mm_nt(s.grad_resid_low[...], w_proj[...]).astype(BF16)
     s.grad_bias[...] = jnp.zeros_like(s.grad_bias)
-
-    def windows_back(first, last):
-        @pl.loop(first, last, unroll=2)
-        def _(w):
-            attend_back(w, s.qkv, s.probs, s.grad_attended, s.grad_bias, s.grad_rows)
-
-    windows_back(0, 2)
-    fc2.first_pieces()
-    fc1.first_halves()
-    windows_back(2, 4)
-    fc1.first_pieces()
-    windows_back(4, 6)
-    s.norm2_z[...] = mm(s.norm1[...], by_z).astype(BF16)
-    s.norm2[...] = mm(s.norm1[...], line_order(False)).astype(BF16)
-    for i in range(3):
-        for left, turned, part in ((0, s.norm2, qkv_y), (256, s.norm2_z, qkv_z)):
+    fc1.rows_send(4, slice(64, 80))
+
+    @pl.loop(0, WINDOWS, unroll=2)
+    def _(w):
+        attend_back(w, s.qkv, s.probs, s.grad_attended, s.grad_bias, s.grad_rows)
+
+    for left, order, part in ((0, s.order_y, qkv_y), (256, s.order_z, qkv_z)):
+        s.turned[...] = mm(s.norm1[...], order[...]).astype(BF16)
+        for i in range(3):
             columns = slice(D * i + left, D * i + left + 256)
-            grad = mm_tn(turned[...], s.grad_rows[:, columns]).astype(BF16)
+            grad = mm_tn(s.turned[...], s.grad_rows[:, columns]).astype(BF16)
             part.own[:, :, :, 16 * i : 16 * i + 16, :] = grad.reshape(2, 4, 4, 16, 256)
-    qkv_y.begin()
-    qkv_z.begin()
+        part.rows_start(0, slice(0, 48))
+    s.grad_norm[...] = mm_nt(s.grad_rows[...], w_qkv[...])
+    qkv_y.rows_send(0, slice(0, 48))
+    qkv_z.rows_send(0, slice(0, 48))
+    collect_table(s.grad_bias, s.shifted, s.table)
+    attention_after(s, gain_attn, grad_grid, small)
+    small[:, 0:256] = s.table[...]
+    held[0] = small[...]
+    shared = share_line(at, copies, "c", held.at[0], pair_slots)
     fc2.second_send()
-    s.grad_norm[...] = mm_nt(s.grad_rows[...], w_qkv[...])
-    qkv_y.first_halves()
-    qkv_z.first_halves()
+    sum_shared(shared, held.at[1], pair_slots)
+    shared = share_line(at, copies, "y", held.at[1], y_slots)
+    went_tokens = shift_back_start(copies, grad_grid, *back_tokens)
     fc1.second_send()
-    attention_after(s, gain_attn, grad_grid, small)
-    went_tokens = shift_back_start(copies, grad_grid, *back_tokens)
-    held[0] = small[...]
-    shared = share_all(at, copies, "c", held.at[0], pair_slots)
-    qkv_y.first_pieces()
-    qkv_z.first_pieces()
-    sum_shared(shared, held.at[1], pair_slots)
-    shared = share_all(at, copies, "y", held.at[1], slots.at[0])
+    sum_shared(shared, held.at[2], y_slots)
+    shared = share_plane(at, copies, held.at[2], plane_slots)
+    qkv_y.plane_send(*qkv_y_lines)
+    qkv_z.plane_send(*qkv_z_lines)
     fc2_lines[0][...] = fc2.finish().astype(BF16).reshape(4, 16, D)
-    fc2_sent = line_send(at, copies, *fc2_lines)
+    fc2_sent = line_send(at, copies, "x", *fc2_lines)
     total = fc1.finish()
-    for x in range(4):
-        rows = [total[16 * i + 4 * x : 16 * i + 4 * x + 4] for i in range(5)]
-        fc1_lines[0][x] = jnp.concatenate(rows + [jnp.zeros((12, D), F32)], axis=0).astype(BF16)
-    fc1_sent = line_send(at, copies, *fc1_lines)
-    qkv_y.second_send()
-    qkv_z.second_send()
-    sum_shared(shared, held.at[2], slots.at[0])
-    shared = share_all(at, copies, "z", held.at[2], slots.at[1])
+    for y in range(4):
+        rows = [total[16 * i + 4 * y : 16 * i + 4 * y + 4] for i in range(5)]
+        fc1_lines[0][y] = jnp.concatenate(rows + [jnp.zeros((12, D), F32)], axis=0).astype(BF16)
+    fc1_sent = line_send(at, copies, "y", *fc1_lines)
     shift_back_finish(went_out, out_grid, back_out[1], back_out[3], output)
-    total = jnp.concatenate([qkv_y.finish(), qkv_z.finish()], axis=1)
-    for x in range(4):
-        rows = [total[16 * i + 4 * x : 16 * i + 4 * x + 4] for i in range(3)]
-        qkv_lines[0][x] = jnp.concatenate(rows + [jnp.zeros((4, D), F32)], axis=0).astype(BF16)
-    qkv_sent = line_send(at, copies, *qkv_lines)
-    sum_shared(shared, held.at[3], slots.at[1])
-    shared = share_all(at, copies, "x", held.at[3], slots.at[2])
     shift_back_finish(went_tokens, grad_grid, back_tokens[1], back_tokens[3], grad_tokens)
-    fc2_total[...] = line_finish(at, fc2_sent, *fc2_lines)
-    fc1_total[...] = line_finish(at, fc1_sent, *fc1_lines)
-    qkv_total[...] = line_finish(at, qkv_sent, *qkv_lines)
-    sum_shared(shared, small_total, slots.at[2])
+    sum_shared(shared, small_total, plane_slots)
+    qkv_total[:, 0:256] = qkv_y.plane_finish(*qkv_y_lines)
+    qkv_total[:, 256:512] = qkv_z.plane_finish(*qkv_z_lines)
+    fc2_total[...] = line_finish(at, fc2_sent, "x", *fc2_lines)
+    fc1_total[...] = line_finish(at, fc1_sent, "y", *fc1_lines)
 
 
 def whole(tokens, cotangent, gain_attn, w_qkv, w_proj, rel, gain_mlp, w_fc1, w_fc2):
     vmem = pl.BlockSpec(memory_space=pltpu.VMEM)
-    copies = 100
+    copies = 120
     return pl.pallas_call(
         whole_kernel,
         out_shape=(
@@ -718,7 +754,7 @@
             jax.ShapeDtypeStruct((16, D), F32),
             jax.ShapeDtypeStruct((32, D), F32),
             jax.ShapeDtypeStruct((16, D), F32),
-            jax.ShapeDtypeStruct((2, 8, D), F32),
+            jax.ShapeDtypeStruct((8, D), F32),
         ),
         in_specs=[vmem] * 5 + [pl.BlockSpec(memory_space=pl.ANY)] * 4,
         out_specs=[vmem] * 6,
@@ -726,18 +762,19 @@
         + [pltpu.VMEM(w.shape, BF16) for w in (w_qkv, w_proj, w_fc1, w_fc2)]
         + [pltpu.SemaphoreType.DMA((4,))]
         + [pltpu.VMEM((8, 48, D), F32)] * 4
-        + [pltpu.VMEM((2, 8, D), F32)]
+        + [pltpu.VMEM((8, D), F32)]
         + [pltpu.SemaphoreType.DMA((copies,))] * 2
         + part_scratch(64, D)
         + part_scratch(80, D)
         + part_scratch(48, 256) * 2
         + line_scratch(16)
         + line_scratch(32)
-        + line_scratch(16)
+        + plane_scratch() * 2
         + [
-            pltpu.VMEM((4, 2, 8, D), F32),
-            pltpu.VMEM((2, 2, 8, D), F32),
-            pltpu.VMEM((3, 4, 2, 8, D), F32),
+            pltpu.VMEM((3, 8, D), F32),
+            pltpu.VMEM((2, 8, D), F32),
+            pltpu.VMEM((4, 8, D), F32),
+            pltpu.VMEM((16, 8, D), F32),
         ]
         + SHIFT_SCRATCH * 2
         + ([pltpu.VMEM((4, 48, D), BF16)] + SHIFT_SCRATCH) * 2,
@@ -760,9 +797,10 @@
         grad_fc1[:, D * i : D * i + D] = fc1_total[4 * i : 4 * i + 4]
     grad_proj[...] = fc1_total[16:20]
     grad_fc2[...] = fc2_total[...]
-    table[...] = small[1][:, 0:225]
-    gain_attn[...] = small[0, 0]
-    gain_mlp[...] = small[0, 1]
+    table[...] = small[:, 0:225]
+    for i in range(2):
+        gain_attn[256 * i : 256 * i + 256] = small[i, 256:512]
+        gain_mlp[256 * i : 256 * i + 256] = small[2 + i, 256:512]
 
 
 def deliver(*results):

time: 84.7 us -> 77.6 us (0.916)
  Pallas kernels: 83.9 us -> 76.7 us
    pallas_call x1, Pallas kernels: 81.6 us -> 74.4 us  [whole(): pl.pallas_call(whole_kernel, out_shape=(jax.ShapeDtypeStruct((8, 48, D),...]
where the time goes in v3:
time: 77.6 us; the launch traced here: 77.4 us
  Pallas kernels  76.7 us (99%)
    pallas_call x1, Pallas kernels, whole(): pl.pallas_call(whole_kernel, out_shape=(jax.ShapeDtypeStruct((8, 48, D),...  74.4 us
    pallas_call x1, Pallas kernels, deliver(): pl.pallas_call(deliver_kernel, out_shape=(jax.ShapeDtypeStruct((8, 48, D)...  2.35 us

profile of v3, /device:TPU:0, one launch (start us, length us, event | category | flops | bytes accessed | tf_op | source)
XLA Modules:
  0.0 77.4 jit_solution(13705009394188933564)
XLA Ops:
  0.6 74.4 %whole_block.1 = (bf16[8,48,512]{2,1,0:T(8,128)(2,1)}, f32[8,48,512]{2,1,0:T(8,128)}, f32[16,512]{1,0:T(8,128)}, f32[32,512]{1,0:T(8,128)}, f32[16,512]{1,0:T(8,128)}, /*index=5*/f32[8,512]{1,0:T(8,128)}) custom-call(bf16[8,48,512]{2,1,0:T(8,128)(2,1)} %tokens.1, bf16[8,48,512]{2,1,0:T(8,128)(2,1)} %cotangent.1, f32[1,512]{1,0:T(1,128)} %bitcast.2, ...), custom_call_target="tpu_custom_call" | custom-call | tf_op jit(solution)/shard_map/whole_block/pallas_call | solution.py:749
  75.0 2.4 %deliver.1 = (bf16[8,48,512]{2,1,0:T(8,128)(2,1)}, f32[8,48,512]{2,1,0:T(8,128)}, f32[4,1536]{1,0:T(4,128)}, f32[4,512]{1,0:T(4,128)}, f32[8,225]{1,0:T(8,128)},...) custom-call(bf16[8,48,512]{2,1,0:T(8,128)(2,1)} %get-tuple-element.15.output, ...), custom_call_target="tpu_custom_call" | custom-call | tf_op jit(solution)/shard_map/deliver/pallas_call | solution.py:808

commit v4 on v3

--- a/solution.py
+++ b/solution.py
@@ -48,7 +48,8 @@
     barrier = pltpu.get_barrier_semaphore()
     others = [moved(at, ("c", 1))]
     others += [moved(at, ("z", i), ("x", j)) for i, j in PLANE]
-    others += [moved(at, ("y", i), ("x", j)) for i, j in PLANE if i]
+    others += [moved(at, ("z", i), ("y", j)) for i, j in PLANE if j]
+    others += [moved(at, ("c", 1), ("x", j)) for j in (1, 2, 3)]
     steps = ((1, 0), (0, 1), (1, 1), (-1, 0), (0, -1), (-1, -1))
     others += [neighbour(*step) for step in steps]
     for other in others:
@@ -81,10 +82,11 @@
 
 
 class Part:
-    def __init__(self, at, copies, axes, own, pair, piece1, piece2):
-        self.at, self.copies = at, copies
-        self.first, self.second = axes
-        self.own, self.pair, self.piece1, self.piece2 = own, pair, piece1, piece2
+    def __init__(self, at, copies, axes, fours, own, pair, piece1, lines, lines_in):
+        self.at, self.copies, self.fours = at, copies, fours
+        self.first, self.second, self.third = axes
+        self.own, self.pair, self.piece1 = own, pair, piece1
+        self.lines, self.lines_in = lines, lines_in
         self.pairs, self.sent = {}, []
 
     def slot(self, step):
@@ -135,122 +137,67 @@
                 )
             )
 
-    def second_send(self):
+    def plane_send(self):
         for copy in self.sent:
             copy.wait()
-        mine = self.pair.at[self.slot(0)]
-
-        @pl.loop(0, 4)
-        def _(i):
-            total = mine[i].astype(F32)
-            for k in range(3):
-                total = total + self.piece1[k, i].astype(F32)
-            mine[i] = total.astype(BF16)
-
-        self.sent = [
-            self.copies.start(
-                mine.at[lax.rem(self.at[self.second] + step, 4)],
-                self.piece2.at[step - 1],
-                moved(self.at, (self.second, step)),
-            )
-            for step in (2, 1, 3)
-        ]
-
-    def finish(self):
-        total = self.pair[self.slot(0), self.at[self.second]].astype(F32)
-        for copy in self.sent:
-            copy.wait()
-        for i in range(3):
-            total = total + self.piece2[i].astype(F32)
-        return total
-
-    def plane_send(self, lines, lines_in):
-        for copy in self.sent:
-            copy.wait()
-        mine = self.slot(0)
+        mine, lines = self.slot(0), self.lines
         for i in range(4):
             total = self.pair[mine, i].astype(F32)
             for k in range(3):
                 total = total + self.piece1[k, i].astype(F32)
-            for x in range(4):
-                rows = [total[16 * k + 4 * x : 16 * k + 4 * x + 4] for k in range(3)]
-                rows = rows + [jnp.zeros((4, total.shape[1]), F32)]
-                lines[i, x] = jnp.concatenate(rows, axis=0).astype(BF16)
+            for k in range(4):
+                rows = total[16 * k : 16 * k + 16]
+                if self.fours:
+                    fours = [total[16 * m + 4 * k : 16 * m + 4 * k + 4] for m in range(4)]
+                    rows = jnp.concatenate(fours, axis=0)
+                lines[i, k] = rows.astype(BF16)
         at = self.at
         self.sent = [
             self.copies.start(
-                lines.at[lax.rem(at[self.second] + i, 4), lax.rem(at["x"] + j, 4)],
-                lines_in.at[4 * i + j - 1],
-                moved(at, (self.second, i), ("x", j)),
+                lines.at[lax.rem(at[self.second] + i, 4), lax.rem(at[self.third] + j, 4)],
+                self.lines_in.at[4 * i + j - 1],
+                moved(at, (self.second, i), (self.third, j)),
             )
             for i, j in PLANE
         ]
 
-    def plane_finish(self, lines, lines_in):
-        total = lines[self.at[self.second], self.at["x"]].astype(F32)
+    def finish(self):
+        total = self.lines[self.at[self.second], self.at[self.third]].astype(F32)
         for copy in self.sent:
             copy.wait()
         for i in range(15):
-            total = total + lines_in[i].astype(F32)
+            total = total + self.lines_in[i].astype(F32)
         return total
 
 
-def part_scratch(rows, columns):
+def part_scratch(columns):
     return [
-        pltpu.VMEM((2, 4, 4, rows, columns), BF16),
-        pltpu.VMEM((4, 4, rows, columns), BF16),
-        pltpu.VMEM((3, 4, rows, columns), BF16),
-        pltpu.VMEM((3, rows, columns), BF16),
+        pltpu.VMEM((2, 4, 4, 64, columns), BF16),
+        pltpu.VMEM((4, 4, 64, columns), BF16),
+        pltpu.VMEM((3, 4, 64, columns), BF16),
+        pltpu.VMEM((4, 4, 16, columns), BF16),
+        pltpu.VMEM((15, 16, columns), BF16),
     ]
 
 
-def line_send(at, copies, axis, lines, lines_in):
+def share(at, copies, axes, held, slots):
+    outer, inner = axes
+    mine = at[outer] * 4 + at[inner]
+    slots[mine] = held[...]
     return [
-        copies.start(
-            lines.at[lax.rem(at[axis] + step, 4)], lines_in.at[step - 1], moved(at, (axis, step))
-        )
-        for step in (2, 1, 3)
+        copies.start(held, slots.at[mine], moved(at, (outer, i), (inner, j)))
+        for i, j in PLANE
+        if i < slots.shape[0] // 4
     ]
-
-
-def line_finish(at, started, axis, lines, lines_in):
-    total = lines[at[axis]].astype(F32)
-    for copy in started:
-        copy.wait()
-    for i in range(3):
-        total = total + lines_in[i].astype(F32)
-    return total
-
-
-def line_scratch(rows):
-    return [pltpu.VMEM((4, rows, D), BF16), pltpu.VMEM((3, rows, D), BF16)]
-
-
-def plane_scratch():
-    return [pltpu.VMEM((4, 4, 16, 256), BF16), pltpu.VMEM((15, 16, 256), BF16)]
-
-
-def share_line(at, copies, axis, held, slots):
-    slots[at[axis]] = held[...]
-    return [
-        copies.start(held, slots.at[at[axis]], moved(at, (axis, step)))
-        for step in range(1, slots.shape[0])
-    ]
-
-
-def share_plane(at, copies, held, slots):
-    mine = at["z"] * 4 + at["x"]
-    slots[mine] = held[...]
-    return [copies.start(held, slots.at[mine], moved(at, ("z", i), ("x", j))) for i, j in PLANE]
 
 
 def sum_shared(started, held, slots):
     for copy in started:
         copy.wait()
-    total = slots[0]
+    total = slots[0].astype(F32)
     for i in range(1, slots.shape[0]):
-        total = total + slots[i]
-    held[...] = total
+        total = total + slots[i].astype(F32)
+    held[...] = total.astype(held.dtype)
 
 
 def shift_in_start(copies, source, rows_in, edge, edge_in):
@@ -372,12 +319,12 @@
 
 
 def line_order(axes):
-    place_of = iota((1, D), 1)
+    place_of = iota((D, 1), 0)
     core, r = place_of >> 8, place_of & 3
     at = {axis: (place_of >> shift) & 3 for axis, shift in zip(axes, (6, 4, 2))}
     z = ((at["z"] & 1) << 6) | ((at["z"] >> 1) << 5)
     feature = (at["y"] << 7) | z | (at["x"] << 3) | (core << 2) | r
-    return jnp.where(iota((D, D), 0) == feature, 1.0, 0.0).astype(BF16)
+    return jnp.where(iota((D, D), 1) == feature, 1.0, 0.0).astype(BF16)
 
 
 def pair_offsets():
@@ -510,10 +457,9 @@
     ("hat2", (TOKENS, D), F32),
     ("factor2", (TOKENS, 128), F32),
     ("norm2", (TOKENS, D), BF16),
-    ("turned", (TOKENS, D), BF16),
-    ("order_fc1", (D, D), BF16),
+    ("turned", (D, TOKENS), BF16),
     ("order_y", (D, D), BF16),
-    ("order_z", (D, D), BF16),
+    ("order_x", (D, D), BF16),
     ("cot", (TOKENS, D), BF16),
     ("hidden", (TOKENS, D), F32),
     ("grad_active", (TOKENS, D), F32),
@@ -569,7 +515,7 @@
         s.cot[rows] = grid_tile(c_grid, i).astype(BF16)
 
     tiles(second_norm)
-    s.turned[...] = mm(s.norm2[...], s.order_fc1[...]).astype(BF16)
+    s.turned[...] = mm_nt(s.order_x[...], s.norm2[...]).astype(BF16)
     s.mlp_out[...] = jnp.zeros_like(s.mlp_out)
     s.grad_norm[...] = jnp.zeros_like(s.grad_norm)
 
@@ -593,7 +539,7 @@
                     own_fc2[c, j, 2 * high + low, 16 * x : 16 * x + 16, :] = grad_fc2[
                         low, high, x, c
                     ]
-    grad_fc1 = mm_tn(s.turned[...], s.grad_hidden[...]).astype(BF16)
+    grad_fc1 = mm(s.turned[...], s.grad_hidden[...]).astype(BF16)
     own_fc1[:, :, :, block, :] = grad_fc1.reshape(2, 4, 4, 16, D)
     s.mlp_out[...] += mm(s.active[...], w_fc2[columns])
     s.grad_norm[...] += mm_nt(s.grad_hidden[...], w_fc1[:, columns])
@@ -623,11 +569,9 @@
         store_grid_tile(grad_grid, i, s.grad_resid[rows] + back)
 
     tiles(first_back)
-    small[:, 256:512] = jnp.zeros((8, 256), F32)
-    for i in range(2):
-        total = jnp.sum(s.gain_sums[i], axis=0, keepdims=True)
-        small[2 * i : 2 * i + 1, 256:512] = total[:, 0:256]
-        small[2 * i + 1 : 2 * i + 2, 256:512] = total[:, 256:512]
+    gains = [jnp.sum(s.gain_sums[i], axis=0, keepdims=True) for i in range(2)]
+    rows = [gain[:, 256 * k : 256 * k + 256] for gain in gains for k in range(2)]
+    small[...] = jnp.concatenate([s.table[...]] + rows + [jnp.zeros((4, 256), F32)], axis=0)
 
 
 def whole_kernel(
@@ -648,12 +592,12 @@
     send_sems, recv_sems = take(2)
     at = place()
     copies = Copies(send_sems, recv_sems)
-    fc2 = Part(at, copies, ("y", "z"), *take(4))
-    fc1 = Part(at, copies, ("x", "z"), *take(4))
-    qkv_y = Part(at, copies, ("y", "z"), *take(4))
-    qkv_z = Part(at, copies, ("z", "y"), *take(4))
-    fc2_lines, fc1_lines, qkv_y_lines, qkv_z_lines = take(2), take(2), take(2), take(2)
-    held, pair_slots, y_slots, plane_slots = take(4)
+    fc2 = Part(at, copies, ("y", "z", "x"), False, *take(5))
+    fc1 = Part(at, copies, ("x", "z", "y"), True, *take(5))
+    rest_y = Part(at, copies, ("y", "z", "x"), True, *take(5))
+    rest_x = Part(at, copies, ("x", "z", "y"), True, *take(5))
+    halves = ((slice(0, 256), s.order_y, rest_y), (slice(256, 512), s.order_x, rest_x))
+    held, pair_slots, plane_slots = take(3)
     in_tokens, in_cot = take(3), take(3)
     back_out, back_tokens = take(4), take(4)
 
@@ -665,9 +609,8 @@
     expand_bias(rel, s.table, s.shifted, s.bias, lax.axis_index("lat") == 0)
     pl.semaphore_wait(pltpu.get_barrier_semaphore(), partners)
     came_tokens = shift_in_start(copies, tokens, *in_tokens)
-    s.order_fc1[...] = line_order(("x", "z", "y"))
     s.order_y[...] = line_order(("y", "z", "x"))
-    s.order_z[...] = line_order(("z", "y", "x"))
+    s.order_x[...] = line_order(("x", "z", "y"))
     shift_in_finish(came_tokens, tokens, in_tokens[0], in_tokens[2], x_grid)
     came_cot = shift_in_start(copies, cotangent, *in_cot)
     loads[0].wait()
@@ -691,70 +634,62 @@
     fc1.rows_send(3, blocks[3])
     fc2.place_send(0)
     went_out = shift_back_start(copies, out_grid, *back_out)
-    s.turned[...] = mm(s.attended[...], s.order_fc1[...]).astype(BF16)
-    grad_proj = mm_tn(s.turned[...], s.grad_resid_low[...]).astype(BF16)
-    fc1.own[:, :, :, 64:80, :] = grad_proj.reshape(2, 4, 4, 16, D)
-    fc1.rows_start(4, slice(64, 80))
+    for columns, order, part in halves:
+        s.turned[...] = mm_nt(order[...], s.attended[...]).astype(BF16)
+        grad_proj = mm(s.turned[...], s.grad_resid_low[:, columns]).astype(BF16)
+        part.own[:, :, :, 48:64, :] = grad_proj.reshape(2, 4, 4, 16, 256)
+        part.rows_start(1, slice(48, 64))
     s.grad_attended[...] = mm_nt(s.grad_resid_low[...], w_proj[...]).astype(BF16)
     s.grad_bias[...] = jnp.zeros_like(s.grad_bias)
-    fc1.rows_send(4, slice(64, 80))
+    rest_y.rows_send(1, slice(48, 64))
+    rest_x.rows_send(1, slice(48, 64))
 
     @pl.loop(0, WINDOWS, unroll=2)
     def _(w):
         attend_back(w, s.qkv, s.probs, s.grad_attended, s.grad_bias, s.grad_rows)
 
-    for left, order, part in ((0, s.order_y, qkv_y), (256, s.order_z, qkv_z)):
-        s.turned[...] = mm(s.norm1[...], order[...]).astype(BF16)
+    for columns, order, part in halves:
+        s.turned[...] = mm_nt(order[...], s.norm1[...]).astype(BF16)
         for i in range(3):
-            columns = slice(D * i + left, D * i + left + 256)
-            grad = mm_tn(s.turned[...], s.grad_rows[:, columns]).astype(BF16)
+            grad_rows = s.grad_rows[:, D * i + columns.start : D * i + columns.stop]
+            grad = mm(s.turned[...], grad_rows).astype(BF16)
             part.own[:, :, :, 16 * i : 16 * i + 16, :] = grad.reshape(2, 4, 4, 16, 256)
         part.rows_start(0, slice(0, 48))
+    fc2.plane_send()
     s.grad_norm[...] = mm_nt(s.grad_rows[...], w_qkv[...])
-    qkv_y.rows_send(0, slice(0, 48))
-    qkv_z.rows_send(0, slice(0, 48))
+    rest_y.rows_send(0, slice(0, 48))
+    rest_x.rows_send(0, slice(0, 48))
+    fc1.plane_send()
     collect_table(s.grad_bias, s.shifted, s.table)
     attention_after(s, gain_attn, grad_grid, small)
-    small[:, 0:256] = s.table[...]
-    held[0] = small[...]
-    shared = share_line(at, copies, "c", held.at[0], pair_slots)
-    fc2.second_send()
+    held[0] = small[...].astype(BF16)
+    shared = share(at, copies, ("c", "x"), held.at[0], pair_slots)
+    went_tokens = shift_back_start(copies, grad_grid, *back_tokens)
     sum_shared(shared, held.at[1], pair_slots)
-    shared = share_line(at, copies, "y", held.at[1], y_slots)
-    went_tokens = shift_back_start(copies, grad_grid, *back_tokens)
-    fc1.second_send()
-    sum_shared(shared, held.at[2], y_slots)
-    shared = share_plane(at, copies, held.at[2], plane_slots)
-    qkv_y.plane_send(*qkv_y_lines)
-    qkv_z.plane_send(*qkv_z_lines)
-    fc2_lines[0][...] = fc2.finish().astype(BF16).reshape(4, 16, D)
-    fc2_sent = line_send(at, copies, "x", *fc2_lines)
-    total = fc1.finish()
-    for y in range(4):
-        rows = [total[16 * i + 4 * y : 16 * i + 4 * y + 4] for i in range(5)]
-        fc1_lines[0][y] = jnp.concatenate(rows + [jnp.zeros((12, D), F32)], axis=0).astype(BF16)
-    fc1_sent = line_send(at, copies, "y", *fc1_lines)
+    shared = share(at, copies, ("z", "y"), held.at[1], plane_slots)
+    rest_y.plane_send()
+    rest_x.plane_send()
     shift_back_finish(went_out, out_grid, back_out[1], back_out[3], output)
+    fc2_total[...] = fc2.finish()
     shift_back_finish(went_tokens, grad_grid, back_tokens[1], back_tokens[3], grad_tokens)
+    fc1_total[...] = fc1.finish()
     sum_shared(shared, small_total, plane_slots)
-    qkv_total[:, 0:256] = qkv_y.plane_finish(*qkv_y_lines)
-    qkv_total[:, 256:512] = qkv_z.plane_finish(*qkv_z_lines)
-    fc2_total[...] = line_finish(at, fc2_sent, "x", *fc2_lines)
-    fc1_total[...] = line_finish(at, fc1_sent, "y", *fc1_lines)
+    qkv_total[:, 0:256] = rest_y.finish()
+    qkv_total[:, 256:512] = rest_x.finish()
 
 
 def whole(tokens, cotangent, gain_attn, w_qkv, w_proj, rel, gain_mlp, w_fc1, w_fc2):
     vmem = pl.BlockSpec(memory_space=pltpu.VMEM)
-    copies = 120
+    copies = 140
     return pl.pallas_call(
         whole_kernel,
         out_shape=(
             jax.ShapeDtypeStruct((8, 48, D), BF16),
             jax.ShapeDtypeStruct((8, 48, D), F32),
             jax.ShapeDtypeStruct((16, D), F32),
-            jax.ShapeDtypeStruct((32, D), F32),
             jax.ShapeDtypeStruct((16, D), F32),
-            jax.ShapeDtypeStruct((8, D), F32),
+            jax.ShapeDtypeStruct((16, D), F32),
+            jax.ShapeDtypeStruct((16, 256), F32),
         ),
         in_specs=[vmem] * 5 + [pl.BlockSpec(memory_space=pl.ANY)] * 4,
         out_specs=[vmem] * 6,
@@ -762,19 +697,14 @@
         + [pltpu.VMEM(w.shape, BF16) for w in (w_qkv, w_proj, w_fc1, w_fc2)]
         + [pltpu.SemaphoreType.DMA((4,))]
         + [pltpu.VMEM((8, 48, D), F32)] * 4
-        + [pltpu.VMEM((8, D), F32)]
+        + [pltpu.VMEM((16, 256), F32)]
         + [pltpu.SemaphoreType.DMA((copies,))] * 2
-        + part_scratch(64, D)
-        + part_scratch(80, D)
-        + part_scratch(48, 256) * 2
-        + line_scratch(16)
-        + line_scratch(32)
-        + plane_scratch() * 2
+        + part_scratch(D) * 2
+        + part_scratch(256) * 2
         + [
-            pltpu.VMEM((3, 8, D), F32),
-            pltpu.VMEM((2, 8, D), F32),
-            pltpu.VMEM((4, 8, D), F32),
-            pltpu.VMEM((16, 8, D), F32),
+            pltpu.VMEM((2, 16, 256), BF16),
+            pltpu.VMEM((8, 16, 256), BF16),
+            pltpu.VMEM((16, 16, 256), BF16),
         ]
         + SHIFT_SCRATCH * 2
         + ([pltpu.VMEM((4, 48, D), BF16)] + SHIFT_SCRATCH) * 2,
@@ -795,12 +725,12 @@
         grad_qkv[:, D * i : D * i + D] = qkv_total[4 * i : 4 * i + 4]
     for i in range(4):
         grad_fc1[:, D * i : D * i + D] = fc1_total[4 * i : 4 * i + 4]
-    grad_proj[...] = fc1_total[16:20]
+    grad_proj[...] = qkv_total[12:16]
     grad_fc2[...] = fc2_total[...]
-    table[...] = small[:, 0:225]
+    table[...] = small[0:8, 0:225]
     for i in range(2):
-        gain_attn[256 * i : 256 * i + 256] = small[i, 256:512]
-        gain_mlp[256 * i : 256 * i + 256] = small[2 + i, 256:512]
+        gain_attn[256 * i : 256 * i + 256] = small[8 + i]
+        gain_mlp[256 * i : 256 * i + 256] = small[10 + i]
 
 
 def deliver(*results):

time: 77.6 us -> 73.4 us (0.946); the launches traced: 77.4 us -> 72.2 us
  Pallas kernels: 76.7 us -> 71.4 us
    pallas_call x1, Pallas kernels: 74.4 us -> 69.1 us  [whole(): pl.pallas_call(whole_kernel, out_shape=(jax.ShapeDtypeStruct((8, 48, D),...]
where the time goes in v4:
time: 73.4 us; the launch traced here: 72.2 us
  Pallas kernels  71.4 us (97%)
  between operations  0.81 us (1%)
    pallas_call x1, Pallas kernels, whole(): pl.pallas_call(whole_kernel, out_shape=(jax.ShapeDtypeStruct((8, 48, D),...  69.1 us
    pallas_call x1, Pallas kernels, deliver(): pl.pallas_call(deliver_kernel, out_shape=(jax.ShapeDtypeStruct((8, 48, D)...  2.35 us

profile of v4, /device:TPU:0, one launch (start us, length us, event | category | flops | bytes accessed | tf_op | source)
XLA Modules:
  0.0 72.2 jit_solution(16852386506750268839)
XLA Ops:
  0.6 69.1 %whole_block.1 = (bf16[8,48,512]{2,1,0:T(8,128)(2,1)}, f32[8,48,512]{2,1,0:T(8,128)}, f32[16,512]{1,0:T(8,128)}, f32[16,512]{1,0:T(8,128)}, f32[16,512]{1,0:T(8,128)}, /*index=5*/f32[16,256]{1,0:T(8,128)}) custom-call(bf16[8,48,512]{2,1,0:T(8,128)(2,1)} %tokens.1, bf16[8,48,512]{2,1,0:T(8,128)(2,1)} %cotangent.1, f32[1,512]{1,0:T(1,128)} %bitcast.2, ...), custom_call_target="tpu_custom_call" | custom-call | tf_op jit(solution)/shard_map/whole_block/pallas_call | solution.py:684
  69.7 2.3 %deliver.1 = (bf16[8,48,512]{2,1,0:T(8,128)(2,1)}, f32[8,48,512]{2,1,0:T(8,128)}, f32[4,1536]{1,0:T(4,128)}, f32[4,512]{1,0:T(4,128)}, f32[8,225]{1,0:T(8,128)},...) custom-call(bf16[8,48,512]{2,1,0:T(8,128)(2,1)} %get-tuple-element.15.output, ...), custom_call_target="tpu_custom_call" | custom-call | tf_op jit(solution)/shard_map/deliver/pallas_call | solution.py:738

commit v5 on v4

--- a/solution.py
+++ b/solution.py
@@ -463,8 +463,8 @@
     ("cot", (TOKENS, D), BF16),
     ("hidden", (TOKENS, D), F32),
     ("grad_active", (TOKENS, D), F32),
-    ("active", (TOKENS, D), BF16),
-    ("grad_hidden", (TOKENS, D), BF16),
+    ("active", (TOKENS, 4 * D), BF16),
+    ("grad_hidden", (TOKENS, 4 * D), BF16),
     ("mlp_out", (TOKENS, D), F32),
     ("grad_norm", (TOKENS, D), F32),
     ("grad_resid", (TOKENS, D), F32),
@@ -516,8 +516,6 @@
 
     tiles(second_norm)
     s.turned[...] = mm_nt(s.order_x[...], s.norm2[...]).astype(BF16)
-    s.mlp_out[...] = jnp.zeros_like(s.mlp_out)
-    s.grad_norm[...] = jnp.zeros_like(s.grad_norm)
 
 
 def mlp_step(s, j, block, w_fc1, w_fc2, own_fc2, own_fc1):
@@ -527,11 +525,11 @@
 
     def bend(_, rows):
         active, slope = gelu_both(s.hidden[rows])
-        s.active[rows] = active.astype(BF16)
-        s.grad_hidden[rows] = (slope * s.grad_active[rows]).astype(BF16)
+        s.active[rows, columns] = active.astype(BF16)
+        s.grad_hidden[rows, columns] = (slope * s.grad_active[rows]).astype(BF16)
 
     tiles(bend)
-    grad_fc2 = mm_tn(s.active[...], s.cot[...]).astype(BF16).reshape(2, 2, 4, 2, 16, D)
+    grad_fc2 = mm_tn(s.active[:, columns], s.cot[...]).astype(BF16).reshape(2, 2, 4, 2, 16, D)
     for low in range(2):
         for high in range(2):
             for x in range(4):
@@ -539,13 +537,21 @@
                     own_fc2[c, j, 2 * high + low, 16 * x : 16 * x + 16, :] = grad_fc2[
                         low, high, x, c
                     ]
-    grad_fc1 = mm(s.turned[...], s.grad_hidden[...]).astype(BF16)
+    grad_fc1 = mm(s.turned[...], s.grad_hidden[:, columns]).astype(BF16)
     own_fc1[:, :, :, block, :] = grad_fc1.reshape(2, 4, 4, 16, D)
-    s.mlp_out[...] += mm(s.active[...], w_fc2[columns])
-    s.grad_norm[...] += mm_nt(s.grad_hidden[...], w_fc1[:, columns])
-
-
-def after_mlp(s, gain_mlp, out_grid):
+
+
+def mlp_result(s, w_fc2, out_grid):
+    s.mlp_out[...] = mm(s.active[...], w_fc2[...])
+
+    def add(i, rows):
+        store_grid_tile(out_grid, i, s.resid[rows] + s.mlp_out[rows])
+
+    tiles(add)
+
+
+def after_mlp(s, gain_mlp, w_fc1):
+    s.grad_norm[...] = mm_nt(s.grad_hidden[...], w_fc1[...])
     s.gain_sums[...] = jnp.zeros_like(s.gain_sums)
 
     def second_back(i, rows):
@@ -556,7 +562,6 @@
         )
         s.grad_resid[rows] = grad_resid
         s.grad_resid_low[rows] = grad_resid.astype(BF16)
-        store_grid_tile(out_grid, i, s.resid[rows] + s.mlp_out[rows])
 
     tiles(second_back)
 
@@ -630,9 +635,10 @@
         if i:
             fc2.place_send(steps[i - 1])
             fc1.rows_send(i - 1, blocks[i - 1])
-    after_mlp(s, gain_mlp, out_grid)
+    after_mlp(s, gain_mlp, w_fc1)
     fc1.rows_send(3, blocks[3])
     fc2.place_send(0)
+    mlp_result(s, w_fc2, out_grid)
     went_out = shift_back_start(copies, out_grid, *back_out)
     for columns, order, part in halves:
         s.turned[...] = mm_nt(order[...], s.attended[...]).astype(BF16)
@@ -648,6 +654,8 @@
     def _(w):
         attend_back(w, s.qkv, s.probs, s.grad_attended, s.grad_bias, s.grad_rows)
 
+    fc2.plane_send()
+    fc1.plane_send()
     for columns, order, part in halves:
         s.turned[...] = mm_nt(order[...], s.norm1[...]).astype(BF16)
         for i in range(3):
@@ -655,11 +663,9 @@
             grad = mm(s.turned[...], grad_rows).astype(BF16)
             part.own[:, :, :, 16 * i : 16 * i + 16, :] = grad.reshape(2, 4, 4, 16, 256)
         part.rows_start(0, slice(0, 48))
-    fc2.plane_send()
     s.grad_norm[...] = mm_nt(s.grad_rows[...], w_qkv[...])
     rest_y.rows_send(0, slice(0, 48))
     rest_x.rows_send(0, slice(0, 48))
-    fc1.plane_send()
     collect_table(s.grad_bias, s.shifted, s.table)
     attention_after(s, gain_attn, grad_grid, small)
     held[0] = small[...].astype(BF16)

time: 73.4 us -> 71.5 us (0.974)
  Pallas kernels: 71.4 us -> 69.3 us
    pallas_call x1, Pallas kernels: 69.1 us -> 66.9 us  [whole(): pl.pallas_call(whole_kernel, out_shape=(jax.ShapeDtypeStruct((8, 48, D),...]
where the time goes in v5:
time: 71.5 us; the launch traced here: 70.1 us
  Pallas kernels  69.3 us (97%)
  between operations  0.81 us (1%)
    pallas_call x1, Pallas kernels, whole(): pl.pallas_call(whole_kernel, out_shape=(jax.ShapeDtypeStruct((8, 48, D),...  66.9 us
    pallas_call x1, Pallas kernels, deliver(): pl.pallas_call(deliver_kernel, out_shape=(jax.ShapeDtypeStruct((8, 48, D)...  2.35 us

profile of v5, /device:TPU:0, one launch (start us, length us, event | category | flops | bytes accessed | tf_op | source)
XLA Modules:
  0.0 70.1 jit_solution(11792845768890744774)
XLA Ops:
  0.6 66.9 %whole_block.1 = (bf16[8,48,512]{2,1,0:T(8,128)(2,1)}, f32[8,48,512]{2,1,0:T(8,128)}, f32[16,512]{1,0:T(8,128)}, f32[16,512]{1,0:T(8,128)}, f32[16,512]{1,0:T(8,128)}, /*index=5*/f32[16,256]{1,0:T(8,128)}) custom-call(bf16[8,48,512]{2,1,0:T(8,128)(2,1)} %tokens.1, bf16[8,48,512]{2,1,0:T(8,128)(2,1)} %cotangent.1, f32[1,512]{1,0:T(1,128)} %bitcast.2, ...), custom_call_target="tpu_custom_call" | custom-call | tf_op jit(solution)/shard_map/whole_block/pallas_call | solution.py:690
  67.6 2.3 %deliver.1 = (bf16[8,48,512]{2,1,0:T(8,128)(2,1)}, f32[8,48,512]{2,1,0:T(8,128)}, f32[4,1536]{1,0:T(4,128)}, f32[4,512]{1,0:T(4,128)}, f32[8,225]{1,0:T(8,128)},...) custom-call(bf16[8,48,512]{2,1,0:T(8,128)(2,1)} %get-tuple-element.15.output, ...), custom_call_target="tpu_custom_call" | custom-call | tf_op jit(solution)/shard_map/deliver/pallas_call | solution.py:744

commit v6 on v5

--- a/solution.py
+++ b/solution.py
@@ -635,11 +635,11 @@
         if i:
             fc2.place_send(steps[i - 1])
             fc1.rows_send(i - 1, blocks[i - 1])
+    mlp_result(s, w_fc2, out_grid)
+    went_out = shift_back_start(copies, out_grid, *back_out)
     after_mlp(s, gain_mlp, w_fc1)
     fc1.rows_send(3, blocks[3])
     fc2.place_send(0)
-    mlp_result(s, w_fc2, out_grid)
-    went_out = shift_back_start(copies, out_grid, *back_out)
     for columns, order, part in halves:
         s.turned[...] = mm_nt(order[...], s.attended[...]).astype(BF16)
         grad_proj = mm(s.turned[...], s.grad_resid_low[:, columns]).astype(BF16)

time: 71.5 us -> 71.5 us (level)
  the two profiles are of different devices: /device:TPU:0 before, /device:TPU:9 now
where the time goes in v6:
time: 71.5 us; the launch traced here: 71.4 us
  Pallas kernels  70.5 us (99%)
  between operations  0.81 us (1%)
    pallas_call x1, Pallas kernels, whole(): pl.pallas_call(whole_kernel, out_shape=(jax.ShapeDtypeStruct((8, 48, D),...  68.2 us
    pallas_call x1, Pallas kernels, deliver(): pl.pallas_call(deliver_kernel, out_shape=(jax.ShapeDtypeStruct((8, 48, D)...  2.35 us

profile of v6, /device:TPU:9, one launch (start us, length us, event | category | flops | bytes accessed | tf_op | source)
XLA Modules:
  0.0 71.4 jit_solution(17766764811311516357)
XLA Ops:
  0.6 68.2 %whole_block.1 = (bf16[8,48,512]{2,1,0:T(8,128)(2,1)}, f32[8,48,512]{2,1,0:T(8,128)}, f32[16,512]{1,0:T(8,128)}, f32[16,512]{1,0:T(8,128)}, f32[16,512]{1,0:T(8,128)}, /*index=5*/f32[16,256]{1,0:T(8,128)}) custom-call(bf16[8,48,512]{2,1,0:T(8,128)(2,1)} %tokens.1, bf16[8,48,512]{2,1,0:T(8,128)(2,1)} %cotangent.1, f32[1,512]{1,0:T(1,128)} %bitcast.2, ...), custom_call_target="tpu_custom_call" | custom-call | tf_op jit(solution)/shard_map/whole_block/pallas_call | solution.py:690
  68.9 2.3 %deliver.1 = (bf16[8,48,512]{2,1,0:T(8,128)(2,1)}, f32[8,48,512]{2,1,0:T(8,128)}, f32[4,1536]{1,0:T(4,128)}, f32[4,512]{1,0:T(4,128)}, f32[8,225]{1,0:T(8,128)},...) custom-call(bf16[8,48,512]{2,1,0:T(8,128)(2,1)} %get-tuple-element.15.output, ...), custom_call_target="tpu_custom_call" | custom-call | tf_op jit(solution)/shard_map/deliver/pallas_call | solution.py:744
